TPU v7x, 128 devices: a whole 4x4x4 slice. The times are simulated.
128 devices in a mesh: seq: 8 (over y_lo, x), tile: 16 (over z, y_hi, core).
Axes of the slice: x: 4, y: 4 (y_hi: 2, y_lo: 2; y = y_hi * 2 + y_lo), z: 4, core: 2. Of those that a mesh axis runs over, the one named last changes fastest.
Arguments:
- transformer_latents: bfloat16 [16, 64, 1024], P('seq', 'tile'), may hold values from -6 to 6
- tile_arrangement: int32 [8, 32], P('seq'), may hold values from 0 to 31, each once within a row
- entry_conv_weight: bfloat16 [3, 3, 3, 16, 384], replicated, may hold values from -0.3125 to 0.3125
- first_norm_gain: float32 [384], replicated, may hold values from 0.1 to 1.9
- first_conv_weight: bfloat16 [3, 3, 3, 384, 384], replicated, may hold values from -0.0625 to 0.0625
- second_norm_gain: float32 [384], replicated, may hold values from 0.1 to 1.9
- second_conv_weight: bfloat16 [3, 3, 3, 384, 384], replicated, may hold values from -0.0625 to 0.0625
- temporal_upscale_weight: bfloat16 [3, 384, 768], replicated, may hold values from -0.1875 to 0.1875
- spatial_upscale_weight: bfloat16 [3, 3, 384, 192], replicated, may hold values from -0.109375 to 0.109375
Outputs:
- decoded: bfloat16 [32, 128, 128, 192], P('seq', 'tile')
Inputs may be any that keep to these rules, and one draw needn't show every extreme that they name: Each row of tile_arrangement lists every number from 0 to 31 exactly once.
All inputs are finite; a program needn't handle non-finite values.
Results may differ from a plain program's by a relative error of at most 0.02.
Values may be sent and summed in bfloat16 or wider, within the bound.
A program may use at most 192 MiB of HBM per device.

v0:
```python
import jax
import jax.numpy as jnp
from jax import lax
from jax.sharding import PartitionSpec as P

BLOCKS = 2


epsilon = 1e-06


def with_halo(cells, sides, width):
    for axis, dim in sides:
        count = lax.axis_size(axis)
        ends = count - 1
        head = lax.slice_in_dim(cells, 0, width, axis=dim)
        tail = lax.slice_in_dim(cells, cells.shape[dim] - width, cells.shape[dim], axis=dim)
        cells = jnp.concatenate(
            [
                lax.ppermute(tail, axis, [(i, (i + 1) % count) for i in range(ends)]),
                cells,
                lax.ppermute(head, axis, [((i + 1) % count, i) for i in range(ends)]),
            ],
            axis=dim,
        )
    return cells


def from_behind(value, axis, steps):
    count = lax.axis_size(axis)
    leading, last = (max(0, -steps), min(count, count - steps))
    return lax.ppermute(value, axis, [(source, source + steps) for source in range(leading, last)])


def causal_conv(extended, weight):
    frames = extended.shape[0] - 2
    strip_rows = extended.shape[1] - 2
    col_count = extended.shape[2]
    padded = jnp.pad(extended, ((0, 0), (0, 0), (1, 1), (0, 0)))
    gathered = jnp.concatenate(
        [padded[:, :, shift_col : shift_col + col_count] for shift_col in range(3)], axis=3
    )
    matrix = weight.reshape(3, 3, 3 * weight.shape[3], weight.shape[4])
    summed = jnp.zeros((frames * strip_rows * col_count, weight.shape[4]), jnp.float32)
    for tap_time in range(3):
        for tap_row in range(3):
            window = gathered[tap_time : tap_time + frames, tap_row : tap_row + strip_rows].reshape(
                -1, matrix.shape[2]
            )
            summed = summed + jnp.dot(
                window, matrix[tap_time, tap_row], preferred_element_type=jnp.float32
            )
    return summed.reshape(frames, strip_rows, col_count, weight.shape[4])


def normed_silu(values, gain):
    widened = values.astype(jnp.float32)
    mean_square = jnp.mean(widened * widened, axis=-1, keepdims=True)
    return jax.nn.silu(widened * lax.rsqrt(mean_square + epsilon) * gain)


def latent_rims(extended):
    return with_halo(extended, (("tile", 1),), 1)


def feature_rims(extended):
    return with_halo(extended, (("tile", 1),), 1)


def with_cache(values, is_later):
    previous = from_behind(values, "seq", 1) * is_later
    return jnp.concatenate([previous, values], axis=0)


def time_conv(extended, temporal_upscale_weight):
    frames = extended.shape[0] - 2
    flat = extended.reshape(extended.shape[0], -1, extended.shape[3])
    summed = jnp.zeros((frames, flat.shape[1], temporal_upscale_weight.shape[2]), jnp.float32)
    for tap_time in range(3):
        summed = summed + jnp.einsum(
            "fpc,cd->fpd",
            flat[tap_time : tap_time + frames],
            temporal_upscale_weight[tap_time],
            preferred_element_type=jnp.float32,
        )
    channels = temporal_upscale_weight.shape[1]
    split = summed.reshape(frames, extended.shape[1], extended.shape[2], 2, channels)
    doubled = jnp.transpose(split, (0, 3, 1, 2, 4)).reshape(
        2 * frames, extended.shape[1], extended.shape[2], channels
    )
    return doubled.astype(jnp.bfloat16)


def upsample_conv(rimmed, spatial_upscale_weight):
    frames, rows_plus, col_count, channels = rimmed.shape
    strip_rows = rows_plus - 2
    taller = jnp.repeat(rimmed, 2, axis=1)[:, 1 : 2 * strip_rows + 3]
    wider = jnp.repeat(taller, 2, axis=2)
    padded = jnp.pad(wider, ((0, 0), (0, 0), (1, 1), (0, 0)))
    gathered = jnp.concatenate(
        [padded[:, :, shift_col : shift_col + 2 * col_count] for shift_col in range(3)], axis=3
    )
    matrix = spatial_upscale_weight.reshape(3, 3 * channels, spatial_upscale_weight.shape[3])
    summed = jnp.zeros(
        (frames * 2 * strip_rows * 2 * col_count, spatial_upscale_weight.shape[3]), jnp.float32
    )
    for tap_row in range(3):
        window = gathered[:, tap_row : tap_row + 2 * strip_rows].reshape(-1, 3 * channels)
        summed = summed + jnp.dot(window, matrix[tap_row], preferred_element_type=jnp.float32)
    return summed.reshape(
        frames, 2 * strip_rows, 2 * col_count, spatial_upscale_weight.shape[3]
    ).astype(jnp.bfloat16)


def local(
    transformer_latents,
    tile_arrangement,
    entry_conv_weight,
    first_norm_gain,
    first_conv_weight,
    second_norm_gain,
    second_conv_weight,
    temporal_upscale_weight,
    spatial_upscale_weight,
):
    position_count, strip_rows, flattened_width = transformer_latents.shape
    chan_latent = entry_conv_weight.shape[3]
    col_count = flattened_width // chan_latent
    own_band = lax.axis_index("tile")
    band_count = lax.axis_size("tile")
    order_row = tile_arrangement[0]
    reach = 0
    span = 2 * reach + 1
    frame_ids = jnp.repeat(jnp.arange(position_count, dtype=jnp.int32), span)
    band_ids = own_band - reach + jnp.tile(jnp.arange(span, dtype=jnp.int32), position_count)
    inside = jnp.logical_and(band_ids >= 0, band_ids < band_count)
    targets = jnp.where(inside, frame_ids * band_count + band_ids, -1)
    select = (order_row[None, :] == targets[:, None]).astype(jnp.bfloat16)
    placed = jnp.einsum(
        "fn,nrx->frx",
        select,
        lax.all_gather(transformer_latents, "tile", axis=0, tiled=True),
        preferred_element_type=jnp.float32,
    )
    latents = placed.astype(jnp.bfloat16).reshape(position_count, -1, col_count, chan_latent)

    def row_mask(values):
        count = values.shape[1]
        rows_global = (
            own_band * strip_rows - (count - strip_rows) // 2 + jnp.arange(count, dtype=jnp.int32)
        )
        valid = jnp.logical_and(rows_global >= 0, rows_global < band_count * strip_rows)
        return values * valid.astype(values.dtype)[None, :, None, None]

    is_later = (lax.axis_index("seq") % BLOCKS != 0).astype(jnp.bfloat16)
    previous = from_behind(latents, "seq", 1) * is_later
    latent_ext = jnp.concatenate([previous, latents], axis=0)
    first = causal_conv(latent_rims(latent_ext), entry_conv_weight).astype(jnp.bfloat16)
    hidden_one = row_mask(normed_silu(first, first_norm_gain).astype(jnp.bfloat16))
    middle = causal_conv(feature_rims(with_cache(hidden_one, is_later)), first_conv_weight)
    hidden_two = row_mask(normed_silu(middle, second_norm_gain).astype(jnp.bfloat16))
    residual_part = first.astype(jnp.float32)
    second = (
        residual_part
        + causal_conv(feature_rims(with_cache(hidden_two, is_later)), second_conv_weight)
    ).astype(jnp.bfloat16)
    second_ext = with_cache(row_mask(second), is_later)
    rimmed = with_halo(time_conv(second_ext, temporal_upscale_weight), (("tile", 1),), 1)
    return upsample_conv(rimmed, spatial_upscale_weight)


def solution(mesh):
    return jax.shard_map(
        local,
        mesh=mesh,
        in_specs=(P("seq", "tile", None), P("seq", None), P(), P(), P(), P(), P(), P(), P()),
        out_specs=P("seq", "tile", None, None),
        check_vma=False,
    )
```

profile of v0, /device:TPU:57, one launch (start us, length us, event | category | flops | bytes accessed | tf_op | source)
XLA Modules:
  0.0 198.3 jit_solution(13475648053575235753)
XLA Ops:
  0.0 20.4 %all_gather.3 = bf16[32,4,1024]{2,1,0:T(4,128)(2,1)S(1)} all-gather(bf16[2,4,1024]{2,1,0:T(4,128)(2,1)} %param.9), channel_id=1, replica_groups=mesh['seq'=8,'tile'=16] {'tile'}, dimensions={0}, use_global_device_ids=true | all-gather | bytes 278528 | tf_op jit(solution)/shard_map/all_gather | solution.py:142
  20.4 0.9 convolution_convert_fusion
  21.5 3.1 %collective-permute-start = (bf16[2,4,64,16]{2,3,1,0:T(8,128)(2,1)S(1)}, bf16[2,4,64,16]{2,3,1,0:T(8,128)(2,1)S(1)}, u32[]{:S(2)}, u32[]{:S(2)}) collective-permute-start(bf16[2,4,64,16]{2,3,1,0:T(8,128)(2,1)S(1)} %copy.48), channel_id=1, source_target_pairs={{0,16},{16,32},{32,48},{48,64},{64,80},{80,96},{96,112},{1,17},{17... | collective-permute-start | bytes 49160 | tf_op jit(solution)/shard_map/ppermute | solution.py:32
  24.7 3.6 %collective-permute-done = bf16[2,4,64,16]{2,3,1,0:T(8,128)(2,1)S(1)} collective-permute-done((bf16[2,4,64,16]{2,3,1,0:T(8,128)(2,1)S(1)}, bf16[2,4,64,16]{2,3,1,0:T(8,128)(2,1)S(1)}, u32[]{:S(2)}, u32[]{:S(2)}) %collective-permute-start) | collective-permute-done | bytes 16416 | tf_op jit(solution)/shard_map/ppermute | solution.py:32
  28.3 6.0 %collective-permute-start.1 = (bf16[4,1,64,16]{2,3,1,0:T(8,128)(2,1)S(1)}, bf16[4,1,64,16]{2,3,1,0:T(8,128)(2,1)S(1)}, u32[]{:S(2)}, u32[]{:S(2)}) collective-permute-start(bf16[4,1,64,16]{2,3,1,0:T(8,128)(2,1)S(1)} %get-tuple-element.52), channel_id=1, source_target_pairs={{0,1},{1,2},{2,3},{3,4},{4,5},{5,6},{6,7},{7,8},{8,9},{9,10},{10,1... | collective-permute-start | bytes 24584 | tf_op jit(solution)/shard_map/ppermute | solution.py:20
  34.3 1.9 collective-permute-start.2
  36.3 5.5 %collective-permute-done.2 = bf16[4,1,64,16]{2,3,1,0:T(8,128)(2,1)S(1)} collective-permute-done((bf16[4,1,64,16]{2,3,1,0:T(8,128)(2,1)S(1)}, bf16[4,1,64,16]{2,3,1,0:T(8,128)(2,1)S(1)}, u32[]{:S(2)}, u32[]{:S(2)}) %collective-permute-start.2) | collective-permute-done | bytes 8224 | tf_op jit(solution)/shard_map/ppermute | solution.py:22
  46.9 1.9 collective-permute-start.3
  48.9 9.8 %collective-permute-done.3 = bf16[2,4,64,384]{3,2,1,0:T(8,128)(2,1)S(1)} collective-permute-done((bf16[2,4,64,384]{3,2,1,0:T(8,128)(2,1)S(1)}, bf16[2,4,64,384]{3,2,1,0:T(8,128)(2,1)S(1)}, u32[]{:S(2)}, u32[]{:S(2)}) %collective-permute-start.3) | collective-permute-done | bytes 393248 | tf_op jit(solution)/shard_map/ppermute | solution.py:32
  58.8 5.5 %collective-permute-start.4 = (bf16[4,1,64,384]{3,2,1,0:T(8,128)(2,1)S(1)}, bf16[4,1,64,384]{3,2,1,0:T(8,128)(2,1)S(1)}, u32[]{:S(2)}, u32[]{:S(2)}) collective-permute-start(bf16[4,1,64,384]{3,2,1,0:T(8,128)(2,1)S(1)} %get-tuple-element.39), channel_id=1, source_target_pairs={{0,1},{1,2},{2,3},{3,4},{4,5},{5,6},{6,7},{7,8},{8,9},{9,10},{10,1... | collective-permute-start | bytes 589832 | tf_op jit(solution)/shard_map/ppermute | solution.py:20
  64.3 1.9 collective-permute-start.5
  66.2 2.1 %collective-permute-done.4 = bf16[4,1,64,384]{3,2,1,0:T(8,128)(2,1)S(1)} collective-permute-done((bf16[4,1,64,384]{3,2,1,0:T(8,128)(2,1)S(1)}, bf16[4,1,64,384]{3,2,1,0:T(8,128)(2,1)S(1)}, u32[]{:S(2)}, u32[]{:S(2)}) %collective-permute-start.4) | collective-permute-done | bytes 196640 | tf_op jit(solution)/shard_map/ppermute | solution.py:20
  68.3 5.3 %collective-permute-done.5 = bf16[4,1,64,384]{3,2,1,0:T(8,128)(2,1)S(1)} collective-permute-done((bf16[4,1,64,384]{3,2,1,0:T(8,128)(2,1)S(1)}, bf16[4,1,64,384]{3,2,1,0:T(8,128)(2,1)S(1)}, u32[]{:S(2)}, u32[]{:S(2)}) %collective-permute-start.5) | collective-permute-done | bytes 196640 | tf_op jit(solution)/shard_map/ppermute | solution.py:22
  73.7 0.6 fusion.10
  74.3 0.7 fusion.72
  75.6 1.2 fusion.69
  77.2 1.3 slice-done.1
  78.5 0.8 fusion.37
  79.3 0.8 fusion.38
  80.1 0.8 fusion.39
  80.9 0.8 fusion.40
  81.7 0.8 fusion.41
  82.5 0.8 fusion.42
  83.3 0.8 fusion.43
  84.1 0.8 fusion.44
  84.9 1.1 multiply_reduce_fusion
  86.5 2.1 %collective-permute-start.6 = (bf16[2,4,64,384]{3,2,1,0:T(8,128)(2,1)S(1)}, bf16[2,4,64,384]{3,2,1,0:T(8,128)(2,1)S(1)}, u32[]{:S(2)}, u32[]{:S(2)}) collective-permute-start(bf16[2,4,64,384]{3,2,1,0:T(8,128)(2,1)S(1)} %fusion.56), channel_id=1, source_target_pairs={{0,16},{16,32},{32,48},{48,64},{64,80},{80,96},{96,112},{1,17},{17... | collective-permute-start | bytes 1179656 | tf_op jit(solution)/shard_map/ppermute | solution.py:32
  88.8 8.5 %collective-permute-done.6 = bf16[2,4,64,384]{3,2,1,0:T(8,128)(2,1)S(1)} collective-permute-done((bf16[2,4,64,384]{3,2,1,0:T(8,128)(2,1)S(1)}, bf16[2,4,64,384]{3,2,1,0:T(8,128)(2,1)S(1)}, u32[]{:S(2)}, u32[]{:S(2)}) %collective-permute-start.6) | collective-permute-done | bytes 393248 | tf_op jit(solution)/shard_map/ppermute | solution.py:32
  97.3 6.7 %collective-permute-start.7 = (bf16[4,1,64,384]{3,2,1,0:T(8,128)(2,1)S(1)}, bf16[4,1,64,384]{3,2,1,0:T(8,128)(2,1)S(1)}, u32[]{:S(2)}, u32[]{:S(2)}) collective-permute-start(bf16[4,1,64,384]{3,2,1,0:T(8,128)(2,1)S(1)} %get-tuple-element.37), channel_id=1, source_target_pairs={{0,1},{1,2},{2,3},{3,4},{4,5},{5,6},{6,7},{7,8},{8,9},{9,10},{10,1... | collective-permute-start | bytes 589832 | tf_op jit(solution)/shard_map/ppermute | solution.py:20
  104.0 1.9 collective-permute-start.8
  106.0 0.6 collective-permute-done.7
  106.6 6.8 %collective-permute-done.8 = bf16[4,1,64,384]{3,2,1,0:T(8,128)(2,1)S(1)} collective-permute-done((bf16[4,1,64,384]{3,2,1,0:T(8,128)(2,1)S(1)}, bf16[4,1,64,384]{3,2,1,0:T(8,128)(2,1)S(1)}, u32[]{:S(2)}, u32[]{:S(2)}) %collective-permute-start.8) | collective-permute-done | bytes 196640 | tf_op jit(solution)/shard_map/ppermute | solution.py:22
  113.4 0.6 select_maximum_fusion
  114.1 0.7 fusion.71
  114.8 0.5 pad_maximum_fusion.2
  115.4 1.2 fusion.68
  117.0 1.3 slice-done.3
  118.3 0.8 fusion.29
  119.1 0.8 fusion.30
  119.9 0.8 fusion.31
  120.7 0.8 fusion.32
  121.5 0.8 fusion.33
  122.3 0.8 fusion.34
  123.1 0.8 fusion.35
  123.9 0.8 fusion.36
  124.7 1.1 fusion.54
  126.0 2.1 %collective-permute-start.9 = (bf16[2,4,64,384]{3,2,1,0:T(8,128)(2,1)S(1)}, bf16[2,4,64,384]{3,2,1,0:T(8,128)(2,1)S(1)}, u32[]{:S(2)}, u32[]{:S(2)}) collective-permute-start(bf16[2,4,64,384]{3,2,1,0:T(8,128)(2,1)S(1)} %fusion.53), channel_id=1, source_target_pairs={{0,16},{16,32},{32,48},{48,64},{64,80},{80,96},{96,112},{1,17},{17... | collective-permute-start | bytes 1179656 | tf_op jit(solution)/shard_map/ppermute | solution.py:32
  128.1 0.6 fusion.45
  128.7 8.2 %collective-permute-done.9 = bf16[2,4,64,384]{3,2,1,0:T(8,128)(2,1)S(1)} collective-permute-done((bf16[2,4,64,384]{3,2,1,0:T(8,128)(2,1)S(1)}, bf16[2,4,64,384]{3,2,1,0:T(8,128)(2,1)S(1)}, u32[]{:S(2)}, u32[]{:S(2)}) %collective-permute-start.9) | collective-permute-done | bytes 393248 | tf_op jit(solution)/shard_map/ppermute | solution.py:32
  137.0 0.6 fusion.47
  137.6 0.6 add_convert_fusion
  138.5 5.3 %collective-permute-start.10 = (bf16[4,1,64,384]{3,2,1,0:T(8,128)(2,1)S(1)}, bf16[4,1,64,384]{3,2,1,0:T(8,128)(2,1)S(1)}, u32[]{:S(2)}, u32[]{:S(2)}) collective-permute-start(bf16[4,1,64,384]{3,2,1,0:T(8,128)(2,1)S(1)} %get-tuple-element.35), channel_id=1, source_target_pairs={{0,1},{1,2},{2,3},{3,4},{4,5},{5,6},{6,7},{7,8},{8,9},{9,10},{10,1... | collective-permute-start | bytes 589832 | tf_op jit(solution)/shard_map/ppermute | solution.py:20
  143.8 1.9 collective-permute-start.11
  147.3 0.6 collective-permute-done.10
  147.9 5.3 %collective-permute-done.11 = bf16[4,1,64,384]{3,2,1,0:T(8,128)(2,1)S(1)} collective-permute-done((bf16[4,1,64,384]{3,2,1,0:T(8,128)(2,1)S(1)}, bf16[4,1,64,384]{3,2,1,0:T(8,128)(2,1)S(1)}, u32[]{:S(2)}, u32[]{:S(2)}) %collective-permute-start.11) | collective-permute-done | bytes 196640 | tf_op jit(solution)/shard_map/ppermute | solution.py:22
  154.0 3.7 %broadcast_in_dim.10 = bf16[4,10,64,2,384]{4,3,2,1,0:T(2,128)(2,1)} broadcast(bf16[4,10,64,384]{3,2,1,0:T(8,128)(2,1)S(1)} %slice.404), dimensions={0,1,2,4} | broadcast | bytes 5898240 | tf_op jit(solution)/shard_map/broadcast_in_dim | solution.py:98
  157.7 9.1 %reshape.224 = bf16[4,10,128,384]{3,2,1,0:T(8,128)(2,1)} reshape(bf16[4,10,64,2,384]{4,3,2,1,0:T(2,128)(2,1)} %broadcast_in_dim.10) | data formatting | bytes 7864320 | tf_op jit(solution)/shard_map/reshape | solution.py:98
  166.8 7.4 %pad_slice_fusion.1 = (bf16[4,10,128,384]{3,2,1,0:T(8,128)(2,1)S(1)}, bf16[4,10,128,384]{3,2,1,0:T(8,128)(2,1)S(1)}) fusion(bf16[4,10,128,384]{3,2,1,0:T(8,128)(2,1)} %reshape.224), kind=kLoop, calls=%fused_computation.7 | loop fusion | bytes 11796480 | tf_op jit(solution)/shard_map/slice | solution.py:101
  174.3 1.8 pad_maximum_fusion
  176.0 6.6 %fusion.67 = (bf16[4,8,128,1152]{3,2,1,0:T(8,128)(2,1)S(1)}, bf16[4,8,128,1152]{3,2,1,0:T(8,128)(2,1)S(1)}, bf16[4,8,128,1152]{3,2,1,0:T(8,128)(2,1)}) fusion(bf16[4,10,128,1152]{3,2,1,0:T(8,128)(2,1)S(1)} %pad_maximum_fusion), kind=kLoop, calls=%fused_computation.145 | loop fusion | bytes 56623104 | tf_op jit(solution)/shard_map/slice | solution.py:108
  182.6 6.9 %fusion.76 = f32[4096,192]{0,1:T(8,128)S(1)} fusion(bf16[4096,1152]{1,0:T(8,128)(2,1)} %bitcast.219, bf16[1152,192]{0,1:T(8,128)(2,1)S(1)} %bitcast.234), kind=kOutput, calls=%fused_computation.154 | convolution fusion | flops 1811939328 | bytes 13025280 | tf_op jit(solution)/shard_map/dot_general | solution.py:109
  189.6 3.3 %convolution_add_fusion.1 = f32[4096,192]{0,1:T(8,128)S(1)} fusion(f32[4096,192]{0,1:T(8,128)S(1)} %fusion.76, bf16[4096,1152]{1,0:T(8,128)(2,1)S(1)} %bitcast.218, bf16[1152,192]{0,1:T(8,128)(2,1)S(1)} %bitcast.235), kind=kOutput, calls=%fused_computation.2 | convolution fusion | flops 1812725760 | bytes 16171008 | tf_op jit(solution)/shard_map/dot_general | solution.py:109
  192.9 3.3 %fusion.2 = bf16[24,8,32,128]{3,1,2,0:T(8,128)(2,1)S(1)} fusion(f32[4096,192]{0,1:T(8,128)S(1)} %convolution_add_fusion.1, bf16[4096,1152]{1,0:T(8,128)(2,1)S(1)} %bitcast.217, bf16[1152,192]{0,1:T(8,128)(2,1)S(1)} %bitcast.236), kind=kOutput, calls=%fused_computation.12 | convolution fusion | flops 1813512192 | bytes 14598144 | tf_op jit(solution)/shard_map/dot_general | solution.py:109
  196.5 1.8 copy.63
  (90 shorter events, 10.7 us)
Async XLA Ops:
  21.5 6.8 %collective-permute-start = (bf16[2,4,64,16]{2,3,1,0:T(8,128)(2,1)S(1)}, bf16[2,4,64,16]{2,3,1,0:T(8,128)(2,1)S(1)}, u32[]{:S(2)}, u32[]{:S(2)}) collective-permute-start(bf16[2,4,64,16]{2,3,1,0:T(8,128)(2,1)S(1)} %copy.48), channel_id=1, source_target_pairs={{0,16},{16,32},{32,48},{48,64},{64,80},{80,96},{96,112},{1,17},{17... | collective-permute-start | bytes 49160 | tf_op jit(solution)/shard_map/ppermute | solution.py:32
  28.3 8.0 %collective-permute-start.1 = (bf16[4,1,64,16]{2,3,1,0:T(8,128)(2,1)S(1)}, bf16[4,1,64,16]{2,3,1,0:T(8,128)(2,1)S(1)}, u32[]{:S(2)}, u32[]{:S(2)}) collective-permute-start(bf16[4,1,64,16]{2,3,1,0:T(8,128)(2,1)S(1)} %get-tuple-element.52), channel_id=1, source_target_pairs={{0,1},{1,2},{2,3},{3,4},{4,5},{5,6},{6,7},{7,8},{8,9},{9,10},{10,1... | collective-permute-start | bytes 24584 | tf_op jit(solution)/shard_map/ppermute | solution.py:20
  34.3 7.5 %collective-permute-start.2 = (bf16[4,1,64,16]{2,3,1,0:T(8,128)(2,1)S(1)}, bf16[4,1,64,16]{2,3,1,0:T(8,128)(2,1)S(1)}, u32[]{:S(2)}, u32[]{:S(2)}) collective-permute-start(bf16[4,1,64,16]{2,3,1,0:T(8,128)(2,1)S(1)} %get-tuple-element.53), channel_id=1, source_target_pairs={{1,0},{2,1},{3,2},{4,3},{5,4},{6,5},{7,6},{8,7},{9,8},{10,9},{11,1... | collective-permute-start | bytes 24584 | tf_op jit(solution)/shard_map/ppermute | solution.py:22
  42.2 1.6 copy-start.3
  45.9 0.8 copy-start.4
  46.9 11.8 %collective-permute-start.3 = (bf16[2,4,64,384]{3,2,1,0:T(8,128)(2,1)S(1)}, bf16[2,4,64,384]{3,2,1,0:T(8,128)(2,1)S(1)}, u32[]{:S(2)}, u32[]{:S(2)}) collective-permute-start(bf16[2,4,64,384]{3,2,1,0:T(8,128)(2,1)S(1)} %fusion.55), channel_id=1, source_target_pairs={{0,16},{16,32},{32,48},{48,64},{64,80},{80,96},{96,112},{1,17},{17... | collective-permute-start | bytes 1179656 | tf_op jit(solution)/shard_map/ppermute | solution.py:32
  58.8 9.5 %collective-permute-start.4 = (bf16[4,1,64,384]{3,2,1,0:T(8,128)(2,1)S(1)}, bf16[4,1,64,384]{3,2,1,0:T(8,128)(2,1)S(1)}, u32[]{:S(2)}, u32[]{:S(2)}) collective-permute-start(bf16[4,1,64,384]{3,2,1,0:T(8,128)(2,1)S(1)} %get-tuple-element.39), channel_id=1, source_target_pairs={{0,1},{1,2},{2,3},{3,4},{4,5},{5,6},{6,7},{7,8},{8,9},{9,10},{10,1... | collective-permute-start | bytes 589832 | tf_op jit(solution)/shard_map/ppermute | solution.py:20
  64.3 9.4 %collective-permute-start.5 = (bf16[4,1,64,384]{3,2,1,0:T(8,128)(2,1)S(1)}, bf16[4,1,64,384]{3,2,1,0:T(8,128)(2,1)S(1)}, u32[]{:S(2)}, u32[]{:S(2)}) collective-permute-start(bf16[4,1,64,384]{3,2,1,0:T(8,128)(2,1)S(1)} %get-tuple-element.40), channel_id=1, source_target_pairs={{1,0},{2,1},{3,2},{4,3},{5,4},{6,5},{7,6},{8,7},{9,8},{10,9},{11,1... | collective-permute-start | bytes 589832 | tf_op jit(solution)/shard_map/ppermute | solution.py:22
  75.0 2.2 %slice-start = ((s8[7962624]{0:T(1024)(128)(4,1)}), s8[4194304]{0:T(1024)(128)(4,1)S(1)}, s32[]{:S(2)}) async-start(s8[7962624]{0:T(1024)(128)(4,1)} %bitcast.264), calls=%async_computation | async-start | bytes 8388608
  75.6 2.9 %slice-start.1 = ((s8[7962624]{0:T(1024)(128)(4,1)}), s8[3768320]{0:T(1024)(128)(4,1)S(1)}, s32[]{:S(2)}) async-start(s8[7962624]{0:T(1024)(128)(4,1)} %bitcast.264), calls=%async_computation.1 | async-start | bytes 7536640
  84.9 1.3 copy-start.5
  86.5 10.7 %collective-permute-start.6 = (bf16[2,4,64,384]{3,2,1,0:T(8,128)(2,1)S(1)}, bf16[2,4,64,384]{3,2,1,0:T(8,128)(2,1)S(1)}, u32[]{:S(2)}, u32[]{:S(2)}) collective-permute-start(bf16[2,4,64,384]{3,2,1,0:T(8,128)(2,1)S(1)} %fusion.56), channel_id=1, source_target_pairs={{0,16},{16,32},{32,48},{48,64},{64,80},{80,96},{96,112},{1,17},{17... | collective-permute-start | bytes 1179656 | tf_op jit(solution)/shard_map/ppermute | solution.py:32
  97.3 9.3 %collective-permute-start.7 = (bf16[4,1,64,384]{3,2,1,0:T(8,128)(2,1)S(1)}, bf16[4,1,64,384]{3,2,1,0:T(8,128)(2,1)S(1)}, u32[]{:S(2)}, u32[]{:S(2)}) collective-permute-start(bf16[4,1,64,384]{3,2,1,0:T(8,128)(2,1)S(1)} %get-tuple-element.37), channel_id=1, source_target_pairs={{0,1},{1,2},{2,3},{3,4},{4,5},{5,6},{6,7},{7,8},{8,9},{9,10},{10,1... | collective-permute-start | bytes 589832 | tf_op jit(solution)/shard_map/ppermute | solution.py:20
  104.0 9.4 %collective-permute-start.8 = (bf16[4,1,64,384]{3,2,1,0:T(8,128)(2,1)S(1)}, bf16[4,1,64,384]{3,2,1,0:T(8,128)(2,1)S(1)}, u32[]{:S(2)}, u32[]{:S(2)}) collective-permute-start(bf16[4,1,64,384]{3,2,1,0:T(8,128)(2,1)S(1)} %get-tuple-element.38), channel_id=1, source_target_pairs={{1,0},{2,1},{3,2},{4,3},{5,4},{6,5},{7,6},{8,7},{9,8},{10,9},{11,1... | collective-permute-start | bytes 589832 | tf_op jit(solution)/shard_map/ppermute | solution.py:22
  114.8 2.2 %slice-start.2 = ((s8[7962624]{0:T(1024)(128)(4,1)}), s8[4194304]{0:T(1024)(128)(4,1)S(1)}, s32[]{:S(2)}) async-start(s8[7962624]{0:T(1024)(128)(4,1)} %bitcast.275), calls=%async_computation.2 | async-start | bytes 8388608
  115.3 2.9 %slice-start.3 = ((s8[7962624]{0:T(1024)(128)(4,1)}), s8[3768320]{0:T(1024)(128)(4,1)S(1)}, s32[]{:S(2)}) async-start(s8[7962624]{0:T(1024)(128)(4,1)} %bitcast.275), calls=%async_computation.3 | async-start | bytes 7536640
  125.8 2.3 %copy-start.1 = (bf16[3,384,768]{2,1,0:T(8,128)(2,1)S(1)}, bf16[3,384,768]{2,1,0:T(8,128)(2,1)}, u32[]{:S(2)}) copy-start(bf16[3,384,768]{2,1,0:T(8,128)(2,1)} %param.16) | copy-start | bytes 5308420
  126.0 10.9 %collective-permute-start.9 = (bf16[2,4,64,384]{3,2,1,0:T(8,128)(2,1)S(1)}, bf16[2,4,64,384]{3,2,1,0:T(8,128)(2,1)S(1)}, u32[]{:S(2)}, u32[]{:S(2)}) collective-permute-start(bf16[2,4,64,384]{3,2,1,0:T(8,128)(2,1)S(1)} %fusion.53), channel_id=1, source_target_pairs={{0,16},{16,32},{32,48},{48,64},{64,80},{80,96},{96,112},{1,17},{17... | collective-permute-start | bytes 1179656 | tf_op jit(solution)/shard_map/ppermute | solution.py:32
  138.1 7.6 %copy-start.2 = (bf16[3,3,384,192]{2,3,1,0:T(8,128)(2,1)S(1)}, bf16[3,3,384,192]{2,3,1,0:T(8,128)(2,1)}, u32[]{:S(2)}) copy-start(bf16[3,3,384,192]{2,3,1,0:T(8,128)(2,1)} %param.17) | copy-start | bytes 3981316
  138.5 9.4 %collective-permute-start.10 = (bf16[4,1,64,384]{3,2,1,0:T(8,128)(2,1)S(1)}, bf16[4,1,64,384]{3,2,1,0:T(8,128)(2,1)S(1)}, u32[]{:S(2)}, u32[]{:S(2)}) collective-permute-start(bf16[4,1,64,384]{3,2,1,0:T(8,128)(2,1)S(1)} %get-tuple-element.35), channel_id=1, source_target_pairs={{0,1},{1,2},{2,3},{3,4},{4,5},{5,6},{6,7},{7,8},{8,9},{9,10},{10,1... | collective-permute-start | bytes 589832 | tf_op jit(solution)/shard_map/ppermute | solution.py:20
  143.8 9.4 %collective-permute-start.11 = (bf16[4,1,64,384]{3,2,1,0:T(8,128)(2,1)S(1)}, bf16[4,1,64,384]{3,2,1,0:T(8,128)(2,1)S(1)}, u32[]{:S(2)}, u32[]{:S(2)}) collective-permute-start(bf16[4,1,64,384]{3,2,1,0:T(8,128)(2,1)S(1)} %get-tuple-element.36), channel_id=1, source_target_pairs={{1,0},{2,1},{3,2},{4,3},{5,4},{6,5},{7,6},{8,7},{9,8},{10,9},{11,1... | collective-permute-start | bytes 589832 | tf_op jit(solution)/shard_map/ppermute | solution.py:22
  166.8 7.4 %copy-start = (bf16[4,10,128,384]{3,2,1,0:T(8,128)(2,1)S(1)}, bf16[4,10,128,384]{3,2,1,0:T(8,128)(2,1)}, u32[]{:S(2)}) copy-start(bf16[4,10,128,384]{3,2,1,0:T(8,128)(2,1)} %reshape.224) | copy-start | bytes 11796484
where the time goes:
time: 199 us; the launch traced here: 198 us
  waiting for transfers between devices  56.5 us (28%)
  local copies, waits for them, and re-layouts  41 us (21%)
  starting transfers between devices  40.4 us (20%)
  matrix products  33.7 us (17%)
  blocking collectives  20.4 us (10%)
  other arithmetic  5.6 us (3%)
    ppermute x4, waiting for transfers between devices, from_behind(): lax.ppermute(value, axis, [(source, source + steps) for source in range(l...  30.1 us
    ppermute x4, starting transfers between devices, with_halo(): lax.ppermute(tail, axis, [(i, (i + 1) % count) for i in range(ends)])  23.5 us
    ppermute x4, waiting for transfers between devices, with_halo(): lax.ppermute(head, axis, [((i + 1) % count, i) for i in range(ends)])  23 us
    all_gather x1, blocking collectives, local(): lax.all_gather(transformer_latents, 'tile', axis=0, tiled=True)  20.4 us
    dot_general x27, matrix products, causal_conv(): jnp.dot(window, matrix[tap_time, tap_row], preferred_element_type=jnp.flo...  17.6 us
    dot_general x3, matrix products, upsample_conv(): jnp.dot(window, matrix[tap_row], preferred_element_type=jnp.float32)  13.5 us
    ppermute x4, starting transfers between devices, from_behind(): lax.ppermute(value, axis, [(source, source + steps) for source in range(l...  9.19 us
    reshape x1, local copies, waits for them, and re-layouts, upsample_conv(): wider = jnp.repeat(taller, 2, axis=2)  9.11 us
  transfers between devices with their start and end apart: 12, of which 11 were waited for; matrix products, arithmetic and copies ran while one was open for 1% of the time, Pallas kernels for 0%

commit v1 on v0

v1 whole, which is shorter than its diff:
```python
import functools

import jax
import jax.numpy as jnp
from jax import lax
from jax.experimental import pallas as pl
from jax.experimental.pallas import tpu as pltpu
from jax.sharding import PartitionSpec as P

EPS = 1e-06
MESH = pl.DeviceIdType.MESH
F32 = jnp.float32
BF16 = jnp.bfloat16

FRAMES = 4
BLOCK = 2
ROWS = 4
COLS = 64
LAT = 16
C = 384
CO = 192
BANDS = 16
TALL = ROWS + 2
CELLS = ROWS * COLS


def silu_norm(v, gain):
    mean = jnp.sum(v * v, axis=-1, keepdims=True) * (1.0 / C)
    u = v * lax.rsqrt(mean + EPS) * gain
    return u / (1.0 + jnp.exp(-u))


def column(shape):
    return lax.broadcasted_iota(jnp.int32, shape, 0)


def shifted(h):
    col = column(h.shape)
    left = jnp.where(col == 0, 0.0, pltpu.roll(h, 1, 0))
    right = jnp.where(col == COLS - 1, 0.0, pltpu.roll(h, COLS - 1, 0))
    return left, right


def put_row(ref, t, y, h):
    left, right = shifted(h)
    ref[t, y, :, 0:C] = left.astype(BF16)
    ref[t, y, :, C : 2 * C] = h.astype(BF16)
    ref[t, y, :, 2 * C : 3 * C] = right.astype(BF16)


def stem_kernel(
    lat_ref,
    arr_ref,
    we_hbm,
    g1_ref,
    w1_hbm,
    g2_ref,
    w2_hbm,
    wt_hbm,
    out_ref,
    gath,
    lat4,
    late,
    lhs,
    rlo,
    rhi,
    patch,
    mid,
    first,
    h1,
    h2,
    acc,
    s_ref,
    we,
    w1,
    w2,
    wt,
    wsem,
    gsend,
    grecv,
    psem,
    hsend,
    hrecv,
    ssend,
    srecv,
):
    seq = lax.axis_index("seq")
    band = lax.axis_index("tile")
    half = lax.rem(seq, 2)
    mate = seq + 1 - 2 * half

    loads = []
    for p in range(9):
        loads.append(
            pltpu.make_async_copy(
                we_hbm.at[pl.ds(48 * p, 48)], we.at[pl.ds(64 * p, 48)], wsem.at[p]
            )
        )
    for k in range(3):
        loads.append(
            pltpu.make_async_copy(w1_hbm.at[2 - k], w1.at[:, pl.ds(k * C, C)], wsem.at[9 + k])
        )
    for k in range(3):
        loads.append(
            pltpu.make_async_copy(w2_hbm.at[2 - k], w2.at[:, pl.ds(k * C, C)], wsem.at[12 + k])
        )
    loads.append(pltpu.make_async_copy(wt_hbm, wt, wsem.at[15]))

    barrier = pltpu.get_barrier_semaphore()
    for d in range(1, BANDS):
        pl.semaphore_signal(
            barrier, inc=1, device_id=(seq, lax.rem(band + d, BANDS)), device_id_type=MESH
        )
    pl.semaphore_signal(barrier, inc=1, device_id=(mate, band), device_id_type=MESH)
    for load in loads:
        load.start()
    pl.semaphore_wait(barrier, BANDS)

    pushes = []
    for d in range(1, BANDS):
        pushes.append(
            pltpu.make_async_remote_copy(
                src_ref=lat_ref,
                dst_ref=gath.at[pl.ds(2 * band, 2)],
                send_sem=gsend.at[d],
                recv_sem=grecv.at[d],
                device_id=(seq, lax.rem(band + d, BANDS)),
                device_id_type=MESH,
            )
        )
    for push in pushes:
        push.start()
    gath[pl.ds(2 * band, 2)] = lat_ref[...]

    for p in range(9):
        we[pl.ds(64 * p + 48, 16)] = jnp.zeros((16, C), BF16)
    we[pl.ds(576, 64)] = jnp.zeros((64, C), BF16)
    rlo[0:2] = jnp.zeros((2, 8, COLS, 128), BF16)
    rhi[0:2] = jnp.zeros((2, 8, COLS, 128), BF16)
    s_ref[0:2] = jnp.zeros((2, TALL, COLS, C), BF16)
    spots = []
    for i in range(BLOCK):
        for o in (-1, 0, 1):
            target = i * BANDS + band + o
            spot = jnp.int32(0)
            for n in range(2 * BANDS):
                spot = jnp.where(arr_ref[0, n] == target, n, spot)
            spots.append(spot)

    for push in pushes:
        push.wait_recv()

    has_up = (band > 0).astype(F32)
    has_down = (band < BANDS - 1).astype(F32)
    picked = []
    for i in range(BLOCK):
        above = gath[spots[3 * i]].astype(F32) * has_up
        own = gath[spots[3 * i + 1]].astype(F32)
        below = gath[spots[3 * i + 2]].astype(F32) * has_down
        picked.append(jnp.concatenate([above[2:4], own, below[0:2]], axis=0))
    lat4[half] = jnp.concatenate(picked, axis=0).astype(BF16)
    swap = pltpu.make_async_remote_copy(
        src_ref=lat4.at[half],
        dst_ref=lat4.at[half],
        send_sem=psem.at[0],
        recv_sem=psem.at[1],
        device_id=(mate, band),
        device_id_type=MESH,
    )
    swap.start()
    swap.wait_recv()

    lat = lat4[...].reshape(4 * 8, COLS * LAT).astype(F32)
    lane = lax.broadcasted_iota(jnp.int32, lat.shape, 1)
    late[0] = jnp.where(lane < LAT, 0.0, pltpu.roll(lat, LAT, 1))
    late[1] = lat
    late[2] = jnp.where(lane >= (COLS - 1) * LAT, 0.0, pltpu.roll(lat, (COLS - 1) * LAT, 1))
    spread = (
        lax.rem(lax.broadcasted_iota(jnp.int32, (16, COLS * LAT), 1), 256) // LAT
        == lax.broadcasted_iota(jnp.int32, (16, COLS * LAT), 0)
    ).astype(F32)

    @pl.loop(0, 4 * 8)
    def _(r):
        for e in range(3):
            row = late[e, pl.ds(r, 1), :]
            full = (jnp.broadcast_to(row, (16, COLS * LAT)) * spread).astype(BF16)
            for g in range(4):
                lhs[r, pl.ds(16 * g, 16), 256 * e : 256 * (e + 1)] = full[
                    :, 256 * g : 256 * (g + 1)
                ]

    kk = lax.broadcasted_iota(jnp.int32, (768, 256), 0)
    nn = lax.broadcasted_iota(jnp.int32, (768, 256), 1)
    inside = lax.rem(nn, 128)
    want = jnp.where(
        nn < 128, inside, inside - 64
    )
    place = ((want >= 0) & (want < 48) & (want // LAT == kk // 256) & (lax.rem(want, LAT) == lax.rem(kk, LAT)))
    place = place.astype(F32).astype(BF16)

    @pl.loop(0, 4)
    def _(t):
        r = jnp.dot(
            lhs[pl.ds(8 * t, 8)].reshape(8 * COLS, 768), place, preferred_element_type=F32
        ).astype(BF16)
        rlo[t + 2] = r[:, 0:128].reshape(8, COLS, 128)
        rhi[t + 2] = r[:, 128:256].reshape(8, COLS, 128)

    for load in loads[:9]:
        load.wait()

    @pl.loop(0, 4)
    def _(t):
        taps = [(a, b) for a in range(3) for b in range(3)]
        for q in range(5):
            a, b = taps[2 * q]
            v = rlo[t + a, pl.ds(b, TALL)]
            if 2 * q + 1 < 9:
                a, b = taps[2 * q + 1]
                v = v + rhi[t + a, pl.ds(b, TALL)]
            patch[:, 128 * q : 128 * (q + 1)] = v.reshape(TALL * COLS, 128)
        mid[...] = jnp.dot(patch[...], we[...], preferred_element_type=F32)
        for y in range(TALL):
            v = mid[pl.ds(COLS * y, COLS)].astype(BF16)
            if 1 <= y <= ROWS:
                first[t, pl.ds(COLS * (y - 1), COLS)] = v
            h = silu_norm(v.astype(F32), g1_ref[...])
            if y == 0:
                h = h * has_up
            if y == TALL - 1:
                h = h * has_down
            put_row(h1, t, y, h)

    up = lax.rem(band + BANDS - 1, BANDS)
    down = lax.rem(band + 1, BANDS)

    def conv_step(source, weight, t):
        window = jnp.concatenate(
            [source[t, b : b + ROWS].reshape(CELLS, 3 * C) for b in range(3)], axis=1
        )
        outs = min(3, FRAMES - t)
        r = jnp.dot(window, weight[:, 0 : C * outs], preferred_element_type=F32)
        for k in range(outs):
            part = r[:, C * k : C * (k + 1)]
            if t == 0 or k == 2:
                acc[t + k] = part
            else:
                acc[t + k] += part

    for load in loads[9:12]:
        load.wait()
    halos = []
    for t in range(FRAMES):
        conv_step(h1, w1, t)
        for y in range(ROWS):
            put_row(h2, t, y + 1, silu_norm(acc[t, pl.ds(COLS * y, COLS)], g2_ref[...]))
        pair = []
        for side, (src, dst, to) in enumerate(((1, TALL - 1, up), (ROWS, 0, down))):
            pair.append(
                pltpu.make_async_remote_copy(
                    src_ref=h2.at[t, src, :, pl.ds(C, C)],
                    dst_ref=h2.at[t, dst, :, pl.ds(C, C)],
                    send_sem=hsend.at[t, side],
                    recv_sem=hrecv.at[t, side],
                    device_id=(seq, to),
                    device_id_type=MESH,
                )
            )
        for copy in pair:
            copy.start()
        halos.append(pair)

    for load in loads[12:15]:
        load.wait()
    edges = []
    for t in range(FRAMES):
        for copy in halos[t]:
            copy.wait_recv()
        put_row(h2, t, TALL - 1, h2[t, TALL - 1, :, C : 2 * C].astype(F32) * has_down)
        put_row(h2, t, 0, h2[t, 0, :, C : 2 * C].astype(F32) * has_up)
        conv_step(h2, w2, t)
        total = (acc[t] + first[t].astype(F32)).astype(BF16)
        s_ref[t + 2, 1 : ROWS + 1] = total.reshape(ROWS, COLS, C)
        pair = []
        for side, (src, dst, to) in enumerate(((1, TALL - 1, up), (ROWS, 0, down))):
            pair.append(
                pltpu.make_async_remote_copy(
                    src_ref=s_ref.at[t + 2, src],
                    dst_ref=s_ref.at[t + 2, dst],
                    send_sem=ssend.at[t, side],
                    recv_sem=srecv.at[t, side],
                    device_id=(seq, to),
                    device_id_type=MESH,
                )
            )
        for copy in pair:
            copy.start()
        edges.append(pair)

    loads[15].wait()
    for pair in edges:
        for copy in pair:
            copy.wait_recv()
    for t in range(FRAMES):
        s_ref[t + 2, 0] = (s_ref[t + 2, 0].astype(F32) * has_up).astype(BF16)
        s_ref[t + 2, TALL - 1] = (s_ref[t + 2, TALL - 1].astype(F32) * has_down).astype(BF16)
    for i in range(BLOCK):
        window = jnp.concatenate(
            [s_ref[BLOCK * half + i + a].reshape(TALL * COLS, C) for a in range(3)], axis=1
        )
        r = jnp.dot(window, wt[...], preferred_element_type=F32).astype(BF16)
        out_ref[2 * i] = r[:, 0:C].reshape(TALL, COLS, C)
        out_ref[2 * i + 1] = r[:, C : 2 * C].reshape(TALL, COLS, C)

    for push in pushes:
        push.wait_send()
    swap.wait_send()
    for pair in halos + edges:
        for copy in pair:
            copy.wait_send()


def stem(lat, arr, we, g1, w1, g2, w2, wt):
    vmem = pl.BlockSpec(memory_space=pltpu.VMEM)
    smem = pl.BlockSpec(memory_space=pltpu.SMEM)
    hbm = pl.BlockSpec(memory_space=pl.ANY)
    dma = pltpu.SemaphoreType.DMA
    return pl.pallas_call(
        stem_kernel,
        out_shape=jax.ShapeDtypeStruct((2 * BLOCK, TALL, COLS, C), BF16),
        in_specs=[vmem, smem, hbm, vmem, hbm, vmem, hbm, hbm],
        out_specs=vmem,
        scratch_shapes=[
            pltpu.VMEM((2 * BANDS, ROWS, COLS * LAT), BF16),
            pltpu.VMEM((2, 16, COLS * LAT), BF16),
            pltpu.VMEM((3, 32, COLS * LAT), F32),
            pltpu.VMEM((32, COLS, 768), BF16),
            pltpu.VMEM((6, 8, COLS, 128), BF16),
            pltpu.VMEM((6, 8, COLS, 128), BF16),
            pltpu.VMEM((TALL * COLS, 640), BF16),
            pltpu.VMEM((TALL * COLS, C), F32),
            pltpu.VMEM((FRAMES, CELLS, C), BF16),
            pltpu.VMEM((FRAMES, TALL, COLS, 3 * C), BF16),
            pltpu.VMEM((FRAMES, TALL, COLS, 3 * C), BF16),
            pltpu.VMEM((FRAMES, CELLS, C), F32),
            pltpu.VMEM((FRAMES + 2, TALL, COLS, C), BF16),
            pltpu.VMEM((640, C), BF16),
            pltpu.VMEM((9 * C, 3 * C), BF16),
            pltpu.VMEM((9 * C, 3 * C), BF16),
            pltpu.VMEM((3 * C, 2 * C), BF16),
            dma((16,)),
            dma((BANDS,)),
            dma((BANDS,)),
            dma((2,)),
            dma((FRAMES, 2)),
            dma((FRAMES, 2)),
            dma((FRAMES, 2)),
            dma((FRAMES, 2)),
        ],
        compiler_params=pltpu.CompilerParams(
            collective_id=0, has_side_effects=True, vmem_limit_bytes=56 * 2**20
        ),
        name="stem",
    )(lat, arr, we, g1, w1, g2, w2, wt)


def upsample_kernel(d_ref, w_ref, out_ref, wide, phase, low, high):
    @pl.when(pl.program_id(0) == 0)
    def _():
        spans = (((0,), (1, 2)), ((0, 1), (2,)))
        for py in range(2):
            for px in range(2):
                for dy in range(2):
                    for dx in range(2):
                        total = None
                        for ty in spans[py][dy]:
                            for tx in spans[px][dx]:
                                term = w_ref[3 * ty + tx].astype(F32)
                                total = term if total is None else total + term
                        at = (2 * dy + dx) * C
                        phase[2 * py + px, 0:CO, at : at + C] = total.astype(BF16)
        phase[:, CO:256] = jnp.zeros((4, 256 - CO, 4 * C), BF16)

    frames = d_ref.shape[0]
    for f in range(frames):
        for y in range(TALL):
            h = d_ref[f, y].astype(F32)
            left, right = shifted(h)
            wide[f, y, :, 0:C] = left.astype(BF16)
            wide[f, y, :, C : 2 * C] = d_ref[f, y]
            wide[f, y, :, 2 * C : 3 * C] = right.astype(BF16)
    for py in range(2):
        for px in range(2):
            window = jnp.concatenate(
                [
                    wide[:, py + dy : py + dy + ROWS, :, C * px : C * (px + 2)].reshape(
                        frames * CELLS, 2 * C
                    )
                    for dy in range(2)
                ],
                axis=1,
            )
            r = lax.dot_general(
                window,
                phase[2 * py + px],
                (((1,), (1,)), ((), ())),
                preferred_element_type=F32,
            )
            for f in range(frames):
                for y in range(ROWS):
                    at = (f * ROWS + y) * COLS
                    low[f, y, py, pl.ds(px, COLS, 2), :] = r[at : at + COLS, 0:128]
                    high[f, y, py, pl.ds(px, COLS, 2), :] = r[at : at + COLS, 128:256]
    for f in range(frames):
        for y in range(ROWS):
            for py in range(2):
                out_ref[f, 2 * y + py, :, 0:128] = low[f, y, py].astype(BF16)
                out_ref[f, 2 * y + py, :, 128:CO] = high[f, y, py, :, 0 : CO - 128].astype(BF16)


def upsample(doubled, w):
    frames = 2
    return pl.pallas_call(
        upsample_kernel,
        grid=(2 * BLOCK // frames,),
        out_shape=jax.ShapeDtypeStruct((2 * BLOCK, 2 * ROWS, 2 * COLS, CO), BF16),
        in_specs=[
            pl.BlockSpec((frames, TALL, COLS, C), lambda f: (f, 0, 0, 0)),
            pl.BlockSpec((9, CO, C), lambda f: (0, 0, 0)),
        ],
        out_specs=pl.BlockSpec((frames, 2 * ROWS, 2 * COLS, CO), lambda f: (f, 0, 0, 0)),
        scratch_shapes=[
            pltpu.VMEM((frames, TALL, COLS, 3 * C), BF16),
            pltpu.VMEM((4, 256, 4 * C), BF16),
            pltpu.VMEM((frames, ROWS, 2, 2 * COLS, 128), F32),
            pltpu.VMEM((frames, ROWS, 2, 2 * COLS, 128), F32),
        ],
        compiler_params=pltpu.CompilerParams(vmem_limit_bytes=48 * 2**20),
        name="upsample",
    )(doubled, w)


def local(
    transformer_latents,
    tile_arrangement,
    entry_conv_weight,
    first_norm_gain,
    first_conv_weight,
    second_norm_gain,
    second_conv_weight,
    temporal_upscale_weight,
    spatial_upscale_weight,
):
    doubled = stem(
        transformer_latents,
        tile_arrangement,
        entry_conv_weight.reshape(27 * LAT, C),
        first_norm_gain.reshape(1, C),
        first_conv_weight.reshape(3, 9 * C, C),
        second_norm_gain.reshape(1, C),
        second_conv_weight.reshape(3, 9 * C, C),
        temporal_upscale_weight.reshape(3 * C, 2 * C),
    )
    return upsample(
        doubled, jnp.transpose(spatial_upscale_weight, (0, 1, 3, 2)).reshape(9, CO, C)
    )


def solution(mesh):
    return jax.shard_map(
        local,
        mesh=mesh,
        in_specs=(P("seq", "tile", None), P("seq", None), P(), P(), P(), P(), P(), P(), P()),
        out_specs=P("seq", "tile", None, None),
        check_vma=False,
    )
```

time: 199 us -> 58.9 us (0.30)
  the two profiles are of different devices: /device:TPU:57 before, /device:TPU:1 now
where the time goes in v1:
time: 58.9 us; the launch traced here: 58.7 us
  Pallas kernels  52.7 us (89%)
  local copies, waits for them, and re-layouts  6 us (10%)
    pallas_call x1, Pallas kernels, stem(): pl.pallas_call(stem_kernel, out_shape=jax.ShapeDtypeStruct((2 * BLOCK, TA...  48.1 us
    pallas_call x1, Pallas kernels, upsample(): pl.pallas_call(upsample_kernel, grid=(2 * BLOCK // frames,), out_shape=ja...  4.62 us
    pallas_call x1, local copies, waits for them, and re-layouts, upsample(): pl.pallas_call(upsample_kernel, grid=(2 * BLOCK // frames,), out_shape=ja...  2.27 us
    unnamed x4, local copies, waits for them, and re-layouts  1.27 us
    reshape x1, local copies, waits for them, and re-layouts, local(): first_norm_gain.reshape(1, C)  1.24 us
    reshape x1, local copies, waits for them, and re-layouts, local(): second_norm_gain.reshape(1, C)  1.22 us

profile of v1, /device:TPU:1, one launch (start us, length us, event | category | flops | bytes accessed | tf_op | source)
XLA Modules:
  0.0 58.7 jit_solution(5391141558274941700)
XLA Ops:
  0.0 1.2 %reshape.22.g1_ref = f32[1,384]{1,0:T(1,128)} reshape(f32[384]{0:T(512)} %param.12) | data formatting | bytes 3072 | tf_op jit(solution)/shard_map/reshape | solution.py:459
  1.2 1.2 %reshape.24.g2_ref = f32[1,384]{1,0:T(1,128)} reshape(f32[384]{0:T(512)} %param.14) | data formatting | bytes 3072 | tf_op jit(solution)/shard_map/reshape | solution.py:461
  2.5 0.0 copy-start.1
  2.5 48.1 %stem.1.d_ref = bf16[4,6,64,384]{3,2,1,0:T(8,128)(2,1)} custom-call(bf16[2,4,1024]{2,1,0:T(4,128)(2,1)} %lat_ref.1, s32[1,32]{1,0:T(1,128)} %arr_ref.1, bf16[432,384]{1,0:T(8,128)(2,1)} %bitcast.11, f32[1,384]{1,0:T(1,128)} %reshape.22.g1_ref, bf16[3,3456,384]{2,1,0:T(8,128)(2,1)} %bitcast.8, f32[1,384]{1,0:T(1,128)} %reshape.24.g2_ref, ...), custom_call_target="tpu_custom_call" | custom-call | tf_op jit(solution)/shard_map/stem/pallas_call | solution.py:329
  50.6 0.0 copy-done.1
  50.6 0.0 copy-start
  50.6 1.3 %copy-done = bf16[4,6,64,384]{3,2,1,0:T(8,128)(2,1)S(1)} copy-done((bf16[4,6,64,384]{3,2,1,0:T(8,128)(2,1)S(1)}, bf16[4,6,64,384]{3,2,1,0:T(8,128)(2,1)}, u32[]{:S(2)}) %copy-start) | copy-done | bytes 1179672
  51.8 4.6 %upsample.1 = bf16[4,8,128,192]{3,2,1,0:T(8,128)(2,1)S(1)} custom-call(bf16[4,6,64,384]{3,2,1,0:T(8,128)(2,1)S(1)} %copy-done, bf16[9,192,384]{2,1,0:T(8,128)(2,1)S(1)} %bitcast.7), custom_call_target="tpu_custom_call" | custom-call | tf_op jit(solution)/shard_map/upsample/pallas_call | solution.py:424
  56.5 2.3 %copy.10 = bf16[4,8,128,192]{2,3,1,0:T(8,128)(2,1)} copy(bf16[4,8,128,192]{3,2,1,0:T(8,128)(2,1)S(1)} %upsample.1) | data formatting | bytes 3145728 | tf_op jit(solution)/shard_map/upsample/pallas_call | solution.py:424
Async XLA Ops:
  2.5 48.1 %copy-start.1 = (bf16[3,3,384,192]{2,3,1,0:T(8,128)(2,1)S(1)}, bf16[3,3,384,192]{2,3,1,0:T(8,128)(2,1)}, u32[]{:S(2)}) copy-start(bf16[3,3,384,192]{2,3,1,0:T(8,128)(2,1)} %param.17) | copy-start | bytes 3981316
  50.6 1.3 %copy-start = (bf16[4,6,64,384]{3,2,1,0:T(8,128)(2,1)S(1)}, bf16[4,6,64,384]{3,2,1,0:T(8,128)(2,1)}, u32[]{:S(2)}) copy-start(bf16[4,6,64,384]{3,2,1,0:T(8,128)(2,1)} %stem.1.d_ref) | copy-start | bytes 3538948

commit v2 on v1

--- a/solution.py
+++ b/solution.py
@@ -22,6 +22,7 @@
 BANDS = 16
 TALL = ROWS + 2
 CELLS = ROWS * COLS
+PAIR = 2 * COLS
 
 
 def silu_norm(v, gain):
@@ -168,44 +169,51 @@
         device_id_type=MESH,
     )
     swap.start()
-    swap.wait_recv()
-
-    lat = lat4[...].reshape(4 * 8, COLS * LAT).astype(F32)
-    lane = lax.broadcasted_iota(jnp.int32, lat.shape, 1)
-    late[0] = jnp.where(lane < LAT, 0.0, pltpu.roll(lat, LAT, 1))
-    late[1] = lat
-    late[2] = jnp.where(lane >= (COLS - 1) * LAT, 0.0, pltpu.roll(lat, (COLS - 1) * LAT, 1))
+
     spread = (
         lax.rem(lax.broadcasted_iota(jnp.int32, (16, COLS * LAT), 1), 256) // LAT
         == lax.broadcasted_iota(jnp.int32, (16, COLS * LAT), 0)
     ).astype(F32)
-
-    @pl.loop(0, 4 * 8)
-    def _(r):
-        for e in range(3):
-            row = late[e, pl.ds(r, 1), :]
-            full = (jnp.broadcast_to(row, (16, COLS * LAT)) * spread).astype(BF16)
-            for g in range(4):
-                lhs[r, pl.ds(16 * g, 16), 256 * e : 256 * (e + 1)] = full[
-                    :, 256 * g : 256 * (g + 1)
-                ]
-
     kk = lax.broadcasted_iota(jnp.int32, (768, 256), 0)
     nn = lax.broadcasted_iota(jnp.int32, (768, 256), 1)
-    inside = lax.rem(nn, 128)
-    want = jnp.where(
-        nn < 128, inside, inside - 64
+    want = jnp.where(nn < 128, nn, nn - 128 - 64)
+    place = (
+        (want >= 0)
+        & (want < 48)
+        & (want // LAT == kk // 256)
+        & (lax.rem(want, LAT) == lax.rem(kk, LAT))
     )
-    place = ((want >= 0) & (want < 48) & (want // LAT == kk // 256) & (lax.rem(want, LAT) == lax.rem(kk, LAT)))
     place = place.astype(F32).astype(BF16)
 
-    @pl.loop(0, 4)
-    def _(t):
-        r = jnp.dot(
-            lhs[pl.ds(8 * t, 8)].reshape(8 * COLS, 768), place, preferred_element_type=F32
-        ).astype(BF16)
-        rlo[t + 2] = r[:, 0:128].reshape(8, COLS, 128)
-        rhi[t + 2] = r[:, 128:256].reshape(8, COLS, 128)
+    def relayout(block):
+        lat = lat4[block].astype(F32)
+        lane = lax.broadcasted_iota(jnp.int32, lat.shape, 1)
+        late[0] = jnp.where(lane < LAT, 0.0, pltpu.roll(lat, LAT, 1))
+        late[1] = lat
+        late[2] = jnp.where(lane >= (COLS - 1) * LAT, 0.0, pltpu.roll(lat, (COLS - 1) * LAT, 1))
+
+        @pl.loop(0, 16)
+        def _(r):
+            for e in range(3):
+                row = late[e, pl.ds(r, 1), :]
+                full = (jnp.broadcast_to(row, (16, COLS * LAT)) * spread).astype(BF16)
+                for g in range(4):
+                    lhs[r, pl.ds(16 * g, 16), 256 * e : 256 * (e + 1)] = full[
+                        :, 256 * g : 256 * (g + 1)
+                    ]
+
+        @pl.loop(0, 2)
+        def _(i):
+            r = jnp.dot(
+                lhs[pl.ds(8 * i, 8)].reshape(8 * COLS, 768), place, preferred_element_type=F32
+            ).astype(BF16)
+            t = 2 * block + i
+            rlo[t + 2] = r[:, 0:128].reshape(8, COLS, 128)
+            rhi[t + 2] = r[:, 128:256].reshape(8, COLS, 128)
+
+    relayout(half)
+    swap.wait_recv()
+    relayout(1 - half)
 
     for load in loads[:9]:
         load.wait()
@@ -235,83 +243,133 @@
     up = lax.rem(band + BANDS - 1, BANDS)
     down = lax.rem(band + 1, BANDS)
 
-    def conv_step(source, weight, t):
-        window = jnp.concatenate(
-            [source[t, b : b + ROWS].reshape(CELLS, 3 * C) for b in range(3)], axis=1
-        )
-        outs = min(3, FRAMES - t)
-        r = jnp.dot(window, weight[:, 0 : C * outs], preferred_element_type=F32)
-        for k in range(outs):
-            part = r[:, C * k : C * (k + 1)]
-            if t == 0 or k == 2:
-                acc[t + k] = part
-            else:
-                acc[t + k] += part
-
-    for load in loads[9:12]:
-        load.wait()
-    halos = []
-    for t in range(FRAMES):
-        conv_step(h1, w1, t)
-        for y in range(ROWS):
-            put_row(h2, t, y + 1, silu_norm(acc[t, pl.ds(COLS * y, COLS)], g2_ref[...]))
+    def window(source, t, edge):
+        rows = (0, 3) if edge else (1, 2)
+        return jnp.concatenate(
+            [
+                jnp.concatenate([source[t + i, y + b] for b in range(3)], axis=1)
+                for i in range(2)
+                for y in rows
+            ],
+            axis=0,
+        )
+
+    def early(source, weight, edge):
+        r = jnp.dot(window(source, 0, edge), weight[...], preferred_element_type=F32)
+        acc[0] = r[0:PAIR, 0:C]
+        acc[1] = r[0:PAIR, C : 2 * C] + r[PAIR:, 0:C]
+        acc[2] = r[0:PAIR, 2 * C :] + r[PAIR:, C : 2 * C]
+        acc[3] = r[PAIR:, 2 * C :]
+
+    def late_part(source, weight, edge):
+        r = jnp.dot(window(source, 2, edge), weight[:, 0 : 2 * C], preferred_element_type=F32)
+        acc[2] += r[0:PAIR, 0:C]
+        acc[3] += r[0:PAIR, C:] + r[PAIR:, 0:C]
+
+    def activate(t, edge):
+        for i in range(2):
+            for k, y in enumerate((0, 3) if edge else (1, 2)):
+                put_row(
+                    h2,
+                    t + i,
+                    y + 1,
+                    silu_norm(acc[t + i, pl.ds(COLS * k, COLS)], g2_ref[...]),
+                )
+
+    def finish(t, edge):
+        for i in range(2):
+            for k, y in enumerate((0, 3) if edge else (1, 2)):
+                total = acc[t + i, pl.ds(COLS * k, COLS)] + first[
+                    t + i, pl.ds(COLS * y, COLS)
+                ].astype(F32)
+                s_ref[t + i + 2, y + 1] = total.astype(BF16)
+
+    def push_rows(ref, t, lanes, sends, recvs):
         pair = []
         for side, (src, dst, to) in enumerate(((1, TALL - 1, up), (ROWS, 0, down))):
             pair.append(
                 pltpu.make_async_remote_copy(
-                    src_ref=h2.at[t, src, :, pl.ds(C, C)],
-                    dst_ref=h2.at[t, dst, :, pl.ds(C, C)],
-                    send_sem=hsend.at[t, side],
-                    recv_sem=hrecv.at[t, side],
+                    src_ref=ref.at[pl.ds(t, 2), src, :, lanes],
+                    dst_ref=ref.at[pl.ds(t, 2), dst, :, lanes],
+                    send_sem=sends.at[t // 2, side],
+                    recv_sem=recvs.at[t // 2, side],
                     device_id=(seq, to),
                     device_id_type=MESH,
                 )
             )
         for copy in pair:
             copy.start()
-        halos.append(pair)
+        return pair
+
+    for load in loads[9:12]:
+        load.wait()
+    middle = pl.ds(C, C)
+    early(h1, w1, True)
+    activate(0, True)
+    halos = [push_rows(h2, 0, middle, hsend, hrecv)]
+    late_part(h1, w1, True)
+    activate(2, True)
+    halos.append(push_rows(h2, 2, middle, hsend, hrecv))
+    early(h1, w1, False)
+    activate(0, False)
+    late_part(h1, w1, False)
+    activate(2, False)
 
     for load in loads[12:15]:
         load.wait()
-    edges = []
-    for t in range(FRAMES):
-        for copy in halos[t]:
+
+    def take_halo(t):
+        for copy in halos[t // 2]:
             copy.wait_recv()
-        put_row(h2, t, TALL - 1, h2[t, TALL - 1, :, C : 2 * C].astype(F32) * has_down)
-        put_row(h2, t, 0, h2[t, 0, :, C : 2 * C].astype(F32) * has_up)
-        conv_step(h2, w2, t)
-        total = (acc[t] + first[t].astype(F32)).astype(BF16)
-        s_ref[t + 2, 1 : ROWS + 1] = total.reshape(ROWS, COLS, C)
-        pair = []
-        for side, (src, dst, to) in enumerate(((1, TALL - 1, up), (ROWS, 0, down))):
-            pair.append(
-                pltpu.make_async_remote_copy(
-                    src_ref=s_ref.at[t + 2, src],
-                    dst_ref=s_ref.at[t + 2, dst],
-                    send_sem=ssend.at[t, side],
-                    recv_sem=srecv.at[t, side],
-                    device_id=(seq, to),
-                    device_id_type=MESH,
+        for i in range(2):
+            put_row(h2, t + i, 0, h2[t + i, 0, :, C : 2 * C].astype(F32) * has_up)
+            put_row(
+                h2, t + i, TALL - 1, h2[t + i, TALL - 1, :, C : 2 * C].astype(F32) * has_down
+            )
+
+    whole = pl.ds(0, C)
+    take_halo(0)
+    early(h2, w2, True)
+    finish(0, True)
+    edges = [push_rows(s_ref.at[pl.ds(2, 4)], 0, whole, ssend, srecv)]
+    take_halo(2)
+    late_part(h2, w2, True)
+    finish(2, True)
+    edges.append(push_rows(s_ref.at[pl.ds(2, 4)], 2, whole, ssend, srecv))
+    early(h2, w2, False)
+    finish(0, False)
+    late_part(h2, w2, False)
+    finish(2, False)
+
+    loads[15].wait()
+
+    def double(rows):
+        cells = len(rows) * COLS
+        stacked = jnp.concatenate(
+            [
+                jnp.concatenate(
+                    [s_ref[BLOCK * half + i + a, y] for a in range(3)], axis=1
                 )
-            )
-        for copy in pair:
-            copy.start()
-        edges.append(pair)
-
-    loads[15].wait()
+                for i in range(BLOCK)
+                for y in rows
+            ],
+            axis=0,
+        )
+        r = jnp.dot(stacked, wt[...], preferred_element_type=F32).astype(BF16)
+        for i in range(BLOCK):
+            for k, y in enumerate(rows):
+                at = i * cells + k * COLS
+                out_ref[2 * i, y] = r[at : at + COLS, 0:C]
+                out_ref[2 * i + 1, y] = r[at : at + COLS, C : 2 * C]
+
+    double(range(1, ROWS + 1))
     for pair in edges:
         for copy in pair:
             copy.wait_recv()
     for t in range(FRAMES):
         s_ref[t + 2, 0] = (s_ref[t + 2, 0].astype(F32) * has_up).astype(BF16)
         s_ref[t + 2, TALL - 1] = (s_ref[t + 2, TALL - 1].astype(F32) * has_down).astype(BF16)
-    for i in range(BLOCK):
-        window = jnp.concatenate(
-            [s_ref[BLOCK * half + i + a].reshape(TALL * COLS, C) for a in range(3)], axis=1
-        )
-        r = jnp.dot(window, wt[...], preferred_element_type=F32).astype(BF16)
-        out_ref[2 * i] = r[:, 0:C].reshape(TALL, COLS, C)
-        out_ref[2 * i + 1] = r[:, C : 2 * C].reshape(TALL, COLS, C)
+    double((0, TALL - 1))
 
     for push in pushes:
         push.wait_send()
@@ -334,8 +392,8 @@
         scratch_shapes=[
             pltpu.VMEM((2 * BANDS, ROWS, COLS * LAT), BF16),
             pltpu.VMEM((2, 16, COLS * LAT), BF16),
-            pltpu.VMEM((3, 32, COLS * LAT), F32),
-            pltpu.VMEM((32, COLS, 768), BF16),
+            pltpu.VMEM((3, 16, COLS * LAT), F32),
+            pltpu.VMEM((16, COLS, 768), BF16),
             pltpu.VMEM((6, 8, COLS, 128), BF16),
             pltpu.VMEM((6, 8, COLS, 128), BF16),
             pltpu.VMEM((TALL * COLS, 640), BF16),
@@ -343,7 +401,7 @@
             pltpu.VMEM((FRAMES, CELLS, C), BF16),
             pltpu.VMEM((FRAMES, TALL, COLS, 3 * C), BF16),
             pltpu.VMEM((FRAMES, TALL, COLS, 3 * C), BF16),
-            pltpu.VMEM((FRAMES, CELLS, C), F32),
+            pltpu.VMEM((FRAMES, PAIR, C), F32),
             pltpu.VMEM((FRAMES + 2, TALL, COLS, C), BF16),
             pltpu.VMEM((640, C), BF16),
             pltpu.VMEM((9 * C, 3 * C), BF16),
@@ -353,10 +411,10 @@
             dma((BANDS,)),
             dma((BANDS,)),
             dma((2,)),
-            dma((FRAMES, 2)),
-            dma((FRAMES, 2)),
-            dma((FRAMES, 2)),
-            dma((FRAMES, 2)),
+            dma((2, 2)),
+            dma((2, 2)),
+            dma((2, 2)),
+            dma((2, 2)),
         ],
         compiler_params=pltpu.CompilerParams(
             collective_id=0, has_side_effects=True, vmem_limit_bytes=56 * 2**20
@@ -415,8 +473,8 @@
     for f in range(frames):
         for y in range(ROWS):
             for py in range(2):
-                out_ref[f, 2 * y + py, :, 0:128] = low[f, y, py].astype(BF16)
-                out_ref[f, 2 * y + py, :, 128:CO] = high[f, y, py, :, 0 : CO - 128].astype(BF16)
+                out_ref[f, 2 * y + py, 0:128] = low[f, y, py].T.astype(BF16)
+                out_ref[f, 2 * y + py, 128:CO] = high[f, y, py].T[0 : CO - 128].astype(BF16)
 
 
 def upsample(doubled, w):
@@ -424,19 +482,19 @@
     return pl.pallas_call(
         upsample_kernel,
         grid=(2 * BLOCK // frames,),
-        out_shape=jax.ShapeDtypeStruct((2 * BLOCK, 2 * ROWS, 2 * COLS, CO), BF16),
+        out_shape=jax.ShapeDtypeStruct((2 * BLOCK, 2 * ROWS, CO, 2 * COLS), BF16),
         in_specs=[
             pl.BlockSpec((frames, TALL, COLS, C), lambda f: (f, 0, 0, 0)),
             pl.BlockSpec((9, CO, C), lambda f: (0, 0, 0)),
         ],
-        out_specs=pl.BlockSpec((frames, 2 * ROWS, 2 * COLS, CO), lambda f: (f, 0, 0, 0)),
+        out_specs=pl.BlockSpec((frames, 2 * ROWS, CO, 2 * COLS), lambda f: (f, 0, 0, 0)),
         scratch_shapes=[
             pltpu.VMEM((frames, TALL, COLS, 3 * C), BF16),
             pltpu.VMEM((4, 256, 4 * C), BF16),
             pltpu.VMEM((frames, ROWS, 2, 2 * COLS, 128), F32),
             pltpu.VMEM((frames, ROWS, 2, 2 * COLS, 128), F32),
         ],
-        compiler_params=pltpu.CompilerParams(vmem_limit_bytes=48 * 2**20),
+        compiler_params=pltpu.CompilerParams(vmem_limit_bytes=60 * 2**20),
         name="upsample",
     )(doubled, w)
 
@@ -456,15 +514,16 @@
         transformer_latents,
         tile_arrangement,
         entry_conv_weight.reshape(27 * LAT, C),
-        first_norm_gain.reshape(1, C),
+        first_norm_gain,
         first_conv_weight.reshape(3, 9 * C, C),
-        second_norm_gain.reshape(1, C),
+        second_norm_gain,
         second_conv_weight.reshape(3, 9 * C, C),
         temporal_upscale_weight.reshape(3 * C, 2 * C),
     )
-    return upsample(
+    decoded = upsample(
         doubled, jnp.transpose(spatial_upscale_weight, (0, 1, 3, 2)).reshape(9, CO, C)
     )
+    return jnp.transpose(decoded, (0, 1, 3, 2))
 
 
 def solution(mesh):

time: 58.9 us -> 51.8 us (0.88)
  local copies, waits for them, and re-layouts: 6 us -> 0 us
  Pallas kernels: 52.7 us -> 51.6 us
    pallas_call x1, Pallas kernels: 48.1 us -> 44.4 us  [stem(): pl.pallas_call(stem_kernel, out_shape=jax.ShapeDtypeStruct((2 * BLOCK, TA...]
    pallas_call x1, Pallas kernels: 4.62 us -> 7.17 us  [upsample(): pl.pallas_call(upsample_kernel, grid=(2 * BLOCK // frames,), out_shape=ja...]
    reshape x2 -> x0, local copies, waits for them, and re-layouts: 2.46 us -> none  [the longest x1 1.24 us: local(): first_norm_gain.reshape(1, C)]
    pallas_call x1 -> x0, local copies, waits for them, and re-layouts: 2.27 us -> none  [upsample(): pl.pallas_call(upsample_kernel, grid=(2 * BLOCK // frames,), out_shape=ja...]
    unnamed x4 -> x0, local copies, waits for them, and re-layouts: 1.27 us -> none
where the time goes in v2:
time: 51.8 us; the launch traced here: 51.6 us
  Pallas kernels  51.6 us (100%)
    pallas_call x1, Pallas kernels, stem(): pl.pallas_call(stem_kernel, out_shape=jax.ShapeDtypeStruct((2 * BLOCK, TA...  44.4 us
    pallas_call x1, Pallas kernels, upsample(): pl.pallas_call(upsample_kernel, grid=(2 * BLOCK // frames,), out_shape=ja...  7.17 us

profile of v2, /device:TPU:1, one launch (start us, length us, event | category | flops | bytes accessed | tf_op | source)
XLA Modules:
  0.0 51.6 jit_solution(4481663115967645744)
XLA Ops:
  0.0 44.4 %stem.1.d_ref = bf16[4,6,64,384]{3,2,1,0:T(8,128)(2,1)} custom-call(bf16[2,4,1024]{2,1,0:T(4,128)(2,1)} %lat_ref.1, s32[1,32]{1,0:T(1,128)} %arr_ref.1, bf16[432,384]{1,0:T(8,128)(2,1)} %bitcast.12, f32[384]{0:T(512)} %g1_ref.1, bf16[3,3456,384]{2,1,0:T(8,128)(2,1)} %bitcast.8, f32[384]{0:T(512)} %g2_ref.1, bf16[3,3456,384]{2,1,0:T(8,128)(2,1)} %bitcast.9, ...), custom_call_target="tpu_custom_call" | custom-call | tf_op jit(solution)/shard_map/stem/pallas_call | solution.py:387
  44.4 7.2 %upsample.1 = bf16[4,8,192,128]{3,2,1,0:T(8,128)(2,1)} custom-call(bf16[4,6,64,384]{3,2,1,0:T(8,128)(2,1)} %stem.1.d_ref, bf16[9,192,384]{2,1,0:T(8,128)(2,1)} %bitcast.11), custom_call_target="tpu_custom_call" | custom-call | tf_op jit(solution)/shard_map/upsample/pallas_call | solution.py:482

commit v3 on v2

--- a/solution.py
+++ b/solution.py
@@ -16,13 +16,12 @@
 BLOCK = 2
 ROWS = 4
 COLS = 64
+HALF = COLS // 2
 LAT = 16
 C = 384
 CO = 192
 BANDS = 16
 TALL = ROWS + 2
-CELLS = ROWS * COLS
-PAIR = 2 * COLS
 
 
 def silu_norm(v, gain):
@@ -31,22 +30,87 @@
     return u / (1.0 + jnp.exp(-u))
 
 
-def column(shape):
-    return lax.broadcasted_iota(jnp.int32, shape, 0)
-
-
-def shifted(h):
-    col = column(h.shape)
-    left = jnp.where(col == 0, 0.0, pltpu.roll(h, 1, 0))
-    right = jnp.where(col == COLS - 1, 0.0, pltpu.roll(h, COLS - 1, 0))
-    return left, right
-
-
-def put_row(ref, t, y, h):
-    left, right = shifted(h)
-    ref[t, y, :, 0:C] = left.astype(BF16)
-    ref[t, y, :, C : 2 * C] = h.astype(BF16)
-    ref[t, y, :, 2 * C : 3 * C] = right.astype(BF16)
+def before(odd):
+    row = lax.broadcasted_iota(jnp.int32, odd.shape, 0)
+    return jnp.where(row == 0, 0.0, pltpu.roll(odd, 1, 0))
+
+
+def after(even):
+    row = lax.broadcasted_iota(jnp.int32, even.shape, 0)
+    return jnp.where(row == HALF - 1, 0.0, pltpu.roll(even, HALF - 1, 0))
+
+
+def put_row(ref, t, y, even, odd):
+    ref[t, y, 0] = (before(odd) - odd).astype(BF16)
+    ref[t, y, 1] = (even + odd).astype(BF16)
+    ref[t, y, 2] = (odd - even).astype(BF16)
+    ref[t, y, 3] = (even - after(even)).astype(BF16)
+
+
+def start_weights(w_hbm, u, sems):
+    copies = []
+    for a in range(3):
+        for e, slot in enumerate((0, 1, 3)):
+            copies.append(
+                pltpu.make_async_copy(
+                    w_hbm.at[a, :, e],
+                    u.at[slot, :, :, pl.ds((2 - a) * C, C)],
+                    sems.at[3 * a + e],
+                )
+            )
+    return copies
+
+
+def combine_weights(u):
+    @pl.loop(0, 3 * (C // 16))
+    def _(i):
+        b, r = i // (C // 16), 16 * lax.rem(i, C // 16)
+        rows = pl.ds(pl.multiple_of(r, 16), 16)
+        outer = (u[0, b, rows].astype(F32) + u[3, b, rows].astype(F32)) * 0.5
+        inner = u[1, b, rows].astype(F32) * 0.5
+        u[1, b, rows] = (outer + inner).astype(BF16)
+        u[2, b, rows] = (outer - inner).astype(BF16)
+
+
+def windows(source, t, frames, k, rows):
+    return jnp.concatenate(
+        [
+            jnp.concatenate([source[t + i, y + b, k] for b in range(3)], axis=1)
+            for i in range(frames)
+            for y in rows
+        ],
+        axis=0,
+    )
+
+
+def conv(source, u, acc, rows):
+    n = HALF * len(rows)
+    for k in range(4):
+        weight = u[k].reshape(3 * C, 3 * C)
+        if len(rows) == 1:
+            r = jnp.dot(windows(source, 0, 4, k, rows), weight, preferred_element_type=F32)
+            q = [r[n * i : n * (i + 1)] for i in range(4)]
+        else:
+            r = jnp.dot(windows(source, 0, 2, k, rows), weight, preferred_element_type=F32)
+            q = [r[0:n], r[n:]]
+            r = jnp.dot(
+                windows(source, 2, 2, k, rows), weight[:, 0 : 2 * C], preferred_element_type=F32
+            )
+            q += [r[0:n], r[n:]]
+        for t in range(FRAMES):
+            part = q[t][:, 0:C]
+            for back in range(1, min(t, 2) + 1):
+                part = part + q[t - back][:, back * C : (back + 1) * C]
+            if k == 0:
+                acc[t, 0, 0:n] = part
+            elif k == 1:
+                acc[t, 0, 0:n] += part
+                acc[t, 1, 0:n] = part
+            elif k == 2:
+                acc[t, 0, 0:n] += part
+                acc[t, 1, 0:n] -= part
+            else:
+                acc[t, 1, 0:n] -= part
 
 
 def stem_kernel(
@@ -72,9 +136,13 @@
     h2,
     acc,
     s_ref,
+    slow_out,
+    slow_in,
+    fast_out,
+    fast_in,
     we,
-    w1,
-    w2,
+    u1,
+    u2,
     wt,
     wsem,
     gsend,
@@ -90,22 +158,18 @@
     half = lax.rem(seq, 2)
     mate = seq + 1 - 2 * half
 
-    loads = []
+    odd_band = lax.rem(band, 2)
+
+    loads1 = start_weights(w1_hbm, u1, wsem.at[pl.ds(0, 9)])
+    loads2 = start_weights(w2_hbm, u2, wsem.at[pl.ds(9, 9)])
+    loads0 = []
     for p in range(9):
-        loads.append(
+        loads0.append(
             pltpu.make_async_copy(
-                we_hbm.at[pl.ds(48 * p, 48)], we.at[pl.ds(64 * p, 48)], wsem.at[p]
+                we_hbm.at[pl.ds(48 * p, 48)], we.at[pl.ds(64 * p, 48)], wsem.at[18 + p]
             )
         )
-    for k in range(3):
-        loads.append(
-            pltpu.make_async_copy(w1_hbm.at[2 - k], w1.at[:, pl.ds(k * C, C)], wsem.at[9 + k])
-        )
-    for k in range(3):
-        loads.append(
-            pltpu.make_async_copy(w2_hbm.at[2 - k], w2.at[:, pl.ds(k * C, C)], wsem.at[12 + k])
-        )
-    loads.append(pltpu.make_async_copy(wt_hbm, wt, wsem.at[15]))
+    load_wt = pltpu.make_async_copy(wt_hbm, wt, wsem.at[27])
 
     barrier = pltpu.get_barrier_semaphore()
     for d in range(1, BANDS):
@@ -113,7 +177,7 @@
             barrier, inc=1, device_id=(seq, lax.rem(band + d, BANDS)), device_id_type=MESH
         )
     pl.semaphore_signal(barrier, inc=1, device_id=(mate, band), device_id_type=MESH)
-    for load in loads:
+    for load in loads1 + loads0 + loads2 + [load_wt]:
         load.start()
     pl.semaphore_wait(barrier, BANDS)
 
@@ -147,6 +211,10 @@
             for n in range(2 * BANDS):
                 spot = jnp.where(arr_ref[0, n] == target, n, spot)
             spots.append(spot)
+
+    for load in loads1:
+        load.wait()
+    combine_weights(u1)
 
     for push in pushes:
         push.wait_recv()
@@ -170,9 +238,10 @@
     )
     swap.start()
 
+    place_of = lax.broadcasted_iota(jnp.int32, (16, COLS * LAT), 0)
+    column_of = 2 * lax.rem(place_of, 8) + place_of // 8
     spread = (
-        lax.rem(lax.broadcasted_iota(jnp.int32, (16, COLS * LAT), 1), 256) // LAT
-        == lax.broadcasted_iota(jnp.int32, (16, COLS * LAT), 0)
+        lax.rem(lax.broadcasted_iota(jnp.int32, (16, COLS * LAT), 1), 256) // LAT == column_of
     ).astype(F32)
     kk = lax.broadcasted_iota(jnp.int32, (768, 256), 0)
     nn = lax.broadcasted_iota(jnp.int32, (768, 256), 1)
@@ -206,16 +275,28 @@
         def _(i):
             r = jnp.dot(
                 lhs[pl.ds(8 * i, 8)].reshape(8 * COLS, 768), place, preferred_element_type=F32
+            )
+            r = jnp.concatenate(
+                [
+                    r[at : at + 8]
+                    for y in range(8)
+                    for par in range(2)
+                    for at in range(y * COLS + 8 * par, (y + 1) * COLS, 16)
+                ],
+                axis=0,
             ).astype(BF16)
             t = 2 * block + i
             rlo[t + 2] = r[:, 0:128].reshape(8, COLS, 128)
             rhi[t + 2] = r[:, 128:256].reshape(8, COLS, 128)
 
     relayout(half)
+    for load in loads2:
+        load.wait()
+    combine_weights(u2)
     swap.wait_recv()
     relayout(1 - half)
 
-    for load in loads[:9]:
+    for load in loads0:
         load.wait()
 
     @pl.loop(0, 4)
@@ -232,116 +313,101 @@
         for y in range(TALL):
             v = mid[pl.ds(COLS * y, COLS)].astype(BF16)
             if 1 <= y <= ROWS:
-                first[t, pl.ds(COLS * (y - 1), COLS)] = v
+                first[t, y - 1] = v
             h = silu_norm(v.astype(F32), g1_ref[...])
             if y == 0:
                 h = h * has_up
             if y == TALL - 1:
                 h = h * has_down
-            put_row(h1, t, y, h)
-
-    up = lax.rem(band + BANDS - 1, BANDS)
-    down = lax.rem(band + 1, BANDS)
-
-    def window(source, t, edge):
-        rows = (0, 3) if edge else (1, 2)
-        return jnp.concatenate(
-            [
-                jnp.concatenate([source[t + i, y + b] for b in range(3)], axis=1)
-                for i in range(2)
-                for y in rows
-            ],
-            axis=0,
+            put_row(h1, t, y, h[0:HALF], h[HALF:])
+
+    far = lax.rem(band + BANDS - 1 + 2 * odd_band, BANDS)
+    near = band + 1 - 2 * odd_band
+    far_inside = jnp.where(odd_band == 0, has_up, has_down)
+    far_row = 3 * odd_band
+    near_row = 3 - far_row
+    far_halo = 5 * odd_band
+    near_halo = 5 - far_halo
+    others = [1 - odd_band + i for i in range(3)]
+
+    def push_to(src, dst, to, send, recv):
+        copy = pltpu.make_async_remote_copy(
+            src_ref=src,
+            dst_ref=dst,
+            send_sem=send,
+            recv_sem=recv,
+            device_id=(seq, to),
+            device_id_type=MESH,
         )
-
-    def early(source, weight, edge):
-        r = jnp.dot(window(source, 0, edge), weight[...], preferred_element_type=F32)
-        acc[0] = r[0:PAIR, 0:C]
-        acc[1] = r[0:PAIR, C : 2 * C] + r[PAIR:, 0:C]
-        acc[2] = r[0:PAIR, 2 * C :] + r[PAIR:, C : 2 * C]
-        acc[3] = r[PAIR:, 2 * C :]
-
-    def late_part(source, weight, edge):
-        r = jnp.dot(window(source, 2, edge), weight[:, 0 : 2 * C], preferred_element_type=F32)
-        acc[2] += r[0:PAIR, 0:C]
-        acc[3] += r[0:PAIR, C:] + r[PAIR:, 0:C]
-
-    def activate(t, edge):
-        for i in range(2):
-            for k, y in enumerate((0, 3) if edge else (1, 2)):
-                put_row(
-                    h2,
-                    t + i,
-                    y + 1,
-                    silu_norm(acc[t + i, pl.ds(COLS * k, COLS)], g2_ref[...]),
-                )
-
-    def finish(t, edge):
-        for i in range(2):
-            for k, y in enumerate((0, 3) if edge else (1, 2)):
-                total = acc[t + i, pl.ds(COLS * k, COLS)] + first[
-                    t + i, pl.ds(COLS * y, COLS)
-                ].astype(F32)
-                s_ref[t + i + 2, y + 1] = total.astype(BF16)
-
-    def push_rows(ref, t, lanes, sends, recvs):
-        pair = []
-        for side, (src, dst, to) in enumerate(((1, TALL - 1, up), (ROWS, 0, down))):
-            pair.append(
-                pltpu.make_async_remote_copy(
-                    src_ref=ref.at[pl.ds(t, 2), src, :, lanes],
-                    dst_ref=ref.at[pl.ds(t, 2), dst, :, lanes],
-                    send_sem=sends.at[t // 2, side],
-                    recv_sem=recvs.at[t // 2, side],
-                    device_id=(seq, to),
-                    device_id_type=MESH,
-                )
-            )
-        for copy in pair:
-            copy.start()
-        return pair
-
-    for load in loads[9:12]:
-        load.wait()
-    middle = pl.ds(C, C)
-    early(h1, w1, True)
-    activate(0, True)
-    halos = [push_rows(h2, 0, middle, hsend, hrecv)]
-    late_part(h1, w1, True)
-    activate(2, True)
-    halos.append(push_rows(h2, 2, middle, hsend, hrecv))
-    early(h1, w1, False)
-    activate(0, False)
-    late_part(h1, w1, False)
-    activate(2, False)
-
-    for load in loads[12:15]:
-        load.wait()
-
-    def take_halo(t):
-        for copy in halos[t // 2]:
-            copy.wait_recv()
-        for i in range(2):
-            put_row(h2, t + i, 0, h2[t + i, 0, :, C : 2 * C].astype(F32) * has_up)
-            put_row(
-                h2, t + i, TALL - 1, h2[t + i, TALL - 1, :, C : 2 * C].astype(F32) * has_down
-            )
-
-    whole = pl.ds(0, C)
-    take_halo(0)
-    early(h2, w2, True)
-    finish(0, True)
-    edges = [push_rows(s_ref.at[pl.ds(2, 4)], 0, whole, ssend, srecv)]
-    take_halo(2)
-    late_part(h2, w2, True)
-    finish(2, True)
-    edges.append(push_rows(s_ref.at[pl.ds(2, 4)], 2, whole, ssend, srecv))
-    early(h2, w2, False)
-    finish(0, False)
-    late_part(h2, w2, False)
-    finish(2, False)
-
-    loads[15].wait()
+        copy.start()
+        return copy
+
+    def activate(t, k, y, out=None):
+        rows = pl.ds(HALF * k, HALF)
+        even = silu_norm(acc[t, 0, rows], g2_ref[...])
+        odd = silu_norm(acc[t, 1, rows], g2_ref[...])
+        put_row(h2, t, y + 1, even, odd)
+        if out is not None:
+            out[t, 0:HALF] = even.astype(BF16)
+            out[t, HALF:] = odd.astype(BF16)
+
+    conv(h1, u1, acc, [far_row])
+    for t in range(FRAMES):
+        activate(t, 0, far_row, slow_out)
+    halos = [push_to(slow_out, slow_in, far, hsend.at[0], hrecv.at[0])]
+    conv(h1, u1, acc, others)
+    for t in range(FRAMES):
+        for k in range(3):
+            activate(t, k, others[k])
+    for t in range(FRAMES):
+        rows = pl.ds(pl.multiple_of(2 * HALF * (1 - odd_band), HALF), HALF)
+        fast_out[t, 0:HALF] = silu_norm(acc[t, 0, rows], g2_ref[...]).astype(BF16)
+        fast_out[t, HALF:] = silu_norm(acc[t, 1, rows], g2_ref[...]).astype(BF16)
+    halos.append(push_to(fast_out, fast_in, near, hsend.at[1], hrecv.at[1]))
+
+    def finish(t, k, y):
+        rows = pl.ds(HALF * k, HALF)
+        for par in range(2):
+            cols = pl.ds(HALF * par, HALF)
+            total = acc[t, par, rows] + first[t, y, cols].astype(F32)
+            s_ref[t + 2, y + 1, cols] = total.astype(BF16)
+
+    halos[0].wait_recv()
+    for t in range(FRAMES):
+        h = slow_in[t].astype(F32) * far_inside
+        put_row(h2, t, far_halo, h[0:HALF], h[HALF:])
+    conv(h2, u2, acc, [far_row])
+    for t in range(FRAMES):
+        finish(t, 0, far_row)
+    frames = pl.ds(2, FRAMES)
+    edges = [
+        push_to(
+            s_ref.at[frames, far_row + 1],
+            s_ref.at[frames, 5 - far_halo],
+            far,
+            ssend.at[0],
+            srecv.at[0],
+        )
+    ]
+    halos[1].wait_recv()
+    for t in range(FRAMES):
+        h = fast_in[t].astype(F32)
+        put_row(h2, t, near_halo, h[0:HALF], h[HALF:])
+    conv(h2, u2, acc, others)
+    for t in range(FRAMES):
+        for k in range(3):
+            finish(t, k, others[k])
+    edges.append(
+        push_to(
+            s_ref.at[frames, near_row + 1],
+            s_ref.at[frames, 5 - near_halo],
+            near,
+            ssend.at[1],
+            srecv.at[1],
+        )
+    )
+
+    load_wt.wait()
 
     def double(rows):
         cells = len(rows) * COLS
@@ -363,20 +429,17 @@
                 out_ref[2 * i + 1, y] = r[at : at + COLS, C : 2 * C]
 
     double(range(1, ROWS + 1))
-    for pair in edges:
-        for copy in pair:
-            copy.wait_recv()
-    for t in range(FRAMES):
-        s_ref[t + 2, 0] = (s_ref[t + 2, 0].astype(F32) * has_up).astype(BF16)
-        s_ref[t + 2, TALL - 1] = (s_ref[t + 2, TALL - 1].astype(F32) * has_down).astype(BF16)
+    for copy in edges:
+        copy.wait_recv()
+    for t in range(FRAMES):
+        s_ref[t + 2, far_halo] = (s_ref[t + 2, far_halo].astype(F32) * far_inside).astype(BF16)
     double((0, TALL - 1))
 
     for push in pushes:
         push.wait_send()
     swap.wait_send()
-    for pair in halos + edges:
-        for copy in pair:
-            copy.wait_send()
+    for copy in halos + edges:
+        copy.wait_send()
 
 
 def stem(lat, arr, we, g1, w1, g2, w2, wt):
@@ -398,23 +461,27 @@
             pltpu.VMEM((6, 8, COLS, 128), BF16),
             pltpu.VMEM((TALL * COLS, 640), BF16),
             pltpu.VMEM((TALL * COLS, C), F32),
-            pltpu.VMEM((FRAMES, CELLS, C), BF16),
-            pltpu.VMEM((FRAMES, TALL, COLS, 3 * C), BF16),
-            pltpu.VMEM((FRAMES, TALL, COLS, 3 * C), BF16),
-            pltpu.VMEM((FRAMES, PAIR, C), F32),
+            pltpu.VMEM((FRAMES, ROWS, COLS, C), BF16),
+            pltpu.VMEM((FRAMES, TALL, 4, HALF, C), BF16),
+            pltpu.VMEM((FRAMES, TALL, 4, HALF, C), BF16),
+            pltpu.VMEM((FRAMES, 2, 3 * HALF, C), F32),
             pltpu.VMEM((FRAMES + 2, TALL, COLS, C), BF16),
+            pltpu.VMEM((FRAMES, COLS, C), BF16),
+            pltpu.VMEM((FRAMES, COLS, C), BF16),
+            pltpu.VMEM((FRAMES, COLS, C), BF16),
+            pltpu.VMEM((FRAMES, COLS, C), BF16),
             pltpu.VMEM((640, C), BF16),
-            pltpu.VMEM((9 * C, 3 * C), BF16),
-            pltpu.VMEM((9 * C, 3 * C), BF16),
+            pltpu.VMEM((4, 3, C, 3 * C), BF16),
+            pltpu.VMEM((4, 3, C, 3 * C), BF16),
             pltpu.VMEM((3 * C, 2 * C), BF16),
-            dma((16,)),
+            dma((28,)),
             dma((BANDS,)),
             dma((BANDS,)),
             dma((2,)),
-            dma((2, 2)),
-            dma((2, 2)),
-            dma((2, 2)),
-            dma((2, 2)),
+            dma((2,)),
+            dma((2,)),
+            dma((2,)),
+            dma((2,)),
         ],
         compiler_params=pltpu.CompilerParams(
             collective_id=0, has_side_effects=True, vmem_limit_bytes=56 * 2**20
@@ -443,21 +510,27 @@
     frames = d_ref.shape[0]
     for f in range(frames):
         for y in range(TALL):
-            h = d_ref[f, y].astype(F32)
-            left, right = shifted(h)
-            wide[f, y, :, 0:C] = left.astype(BF16)
-            wide[f, y, :, C : 2 * C] = d_ref[f, y]
-            wide[f, y, :, 2 * C : 3 * C] = right.astype(BF16)
+            even, odd = d_ref[f, y, 0:HALF], d_ref[f, y, HALF:]
+            wide[f, y, :, 0:C] = before(odd.astype(F32)).astype(BF16)
+            wide[f, y, :, C : 2 * C] = even
+            wide[f, y, :, 2 * C : 3 * C] = odd
+            wide[f, y, :, 3 * C : 4 * C] = after(even.astype(F32)).astype(BF16)
     for py in range(2):
         for px in range(2):
             window = jnp.concatenate(
                 [
-                    wide[:, py + dy : py + dy + ROWS, :, C * px : C * (px + 2)].reshape(
-                        frames * CELLS, 2 * C
+                    jnp.concatenate(
+                        [
+                            wide[f, y + py + dy, :, C * (px + par) : C * (px + par + 2)]
+                            for dy in range(2)
+                        ],
+                        axis=1,
                     )
-                    for dy in range(2)
+                    for f in range(frames)
+                    for y in range(ROWS)
+                    for par in range(2)
                 ],
-                axis=1,
+                axis=0,
             )
             r = lax.dot_general(
                 window,
@@ -467,9 +540,11 @@
             )
             for f in range(frames):
                 for y in range(ROWS):
-                    at = (f * ROWS + y) * COLS
-                    low[f, y, py, pl.ds(px, COLS, 2), :] = r[at : at + COLS, 0:128]
-                    high[f, y, py, pl.ds(px, COLS, 2), :] = r[at : at + COLS, 128:256]
+                    for par in range(2):
+                        at = ((f * ROWS + y) * 2 + par) * HALF
+                        cols = pl.ds(2 * par + px, HALF, 4)
+                        low[f, y, py, cols, :] = r[at : at + HALF, 0:128]
+                        high[f, y, py, cols, :] = r[at : at + HALF, 128:256]
     for f in range(frames):
         for y in range(ROWS):
             for py in range(2):
@@ -489,7 +564,7 @@
         ],
         out_specs=pl.BlockSpec((frames, 2 * ROWS, CO, 2 * COLS), lambda f: (f, 0, 0, 0)),
         scratch_shapes=[
-            pltpu.VMEM((frames, TALL, COLS, 3 * C), BF16),
+            pltpu.VMEM((frames, TALL, HALF, 4 * C), BF16),
             pltpu.VMEM((4, 256, 4 * C), BF16),
             pltpu.VMEM((frames, ROWS, 2, 2 * COLS, 128), F32),
             pltpu.VMEM((frames, ROWS, 2, 2 * COLS, 128), F32),
@@ -515,9 +590,9 @@
         tile_arrangement,
         entry_conv_weight.reshape(27 * LAT, C),
         first_norm_gain,
-        first_conv_weight.reshape(3, 9 * C, C),
+        first_conv_weight,
         second_norm_gain,
-        second_conv_weight.reshape(3, 9 * C, C),
+        second_conv_weight,
         temporal_upscale_weight.reshape(3 * C, 2 * C),
     )
     decoded = upsample(

time: 51.8 us -> 50.9 us (0.983)
  Pallas kernels: 51.6 us -> 50.7 us
    pallas_call x1, Pallas kernels: 44.4 us -> 43.6 us  [stem(): pl.pallas_call(stem_kernel, out_shape=jax.ShapeDtypeStruct((2 * BLOCK, TA...]
where the time goes in v3:
time: 50.9 us; the launch traced here: 50.7 us
  Pallas kernels  50.7 us (100%)
    pallas_call x1, Pallas kernels, stem(): pl.pallas_call(stem_kernel, out_shape=jax.ShapeDtypeStruct((2 * BLOCK, TA...  43.6 us
    pallas_call x1, Pallas kernels, upsample(): pl.pallas_call(upsample_kernel, grid=(2 * BLOCK // frames,), out_shape=ja...  7.16 us

profile of v3, /device:TPU:1, one launch (start us, length us, event | category | flops | bytes accessed | tf_op | source)
XLA Modules:
  0.0 50.7 jit_solution(9758115458873338259)
XLA Ops:
  0.0 43.6 %stem.1.d_ref = bf16[4,6,64,384]{3,2,1,0:T(8,128)(2,1)} custom-call(bf16[2,4,1024]{2,1,0:T(4,128)(2,1)} %lat_ref.1, s32[1,32]{1,0:T(1,128)} %arr_ref.1, bf16[432,384]{1,0:T(8,128)(2,1)} %bitcast.8, f32[384]{0:T(512)} %g1_ref.1, bf16[3,3,3,384,384]{4,3,2,1,0:T(8,128)(2,1)} %w1_hbm.1, f32[384]{0:T(512)} %g2_ref.1, bf16[3,3,3,384,384]{4,3,2,1,0:T(8,128)(2,1)} %w2_hbm.1, ...), custom_call_target="tpu_custom_call" | custom-call | tf_op jit(solution)/shard_map/stem/pallas_call | solution.py:450
  43.6 7.2 %upsample.1 = bf16[4,8,192,128]{3,2,1,0:T(8,128)(2,1)} custom-call(bf16[4,6,64,384]{3,2,1,0:T(8,128)(2,1)} %stem.1.d_ref, bf16[9,192,384]{2,1,0:T(8,128)(2,1)} %bitcast.7), custom_call_target="tpu_custom_call" | custom-call | tf_op jit(solution)/shard_map/upsample/pallas_call | solution.py:557

commit v4 on v3

--- a/solution.py
+++ b/solution.py
@@ -26,8 +26,8 @@
 
 def silu_norm(v, gain):
     mean = jnp.sum(v * v, axis=-1, keepdims=True) * (1.0 / C)
-    u = v * lax.rsqrt(mean + EPS) * gain
-    return u / (1.0 + jnp.exp(-u))
+    w = v * lax.rsqrt(mean + EPS) * gain
+    return w + w * jnp.tanh(w)
 
 
 def before(odd):
@@ -66,10 +66,10 @@
     def _(i):
         b, r = i // (C // 16), 16 * lax.rem(i, C // 16)
         rows = pl.ds(pl.multiple_of(r, 16), 16)
-        outer = (u[0, b, rows].astype(F32) + u[3, b, rows].astype(F32)) * 0.5
-        inner = u[1, b, rows].astype(F32) * 0.5
-        u[1, b, rows] = (outer + inner).astype(BF16)
-        u[2, b, rows] = (outer - inner).astype(BF16)
+        outer = u[0, b, rows] + u[3, b, rows]
+        inner = u[1, b, rows]
+        u[1, b, rows] = (outer + inner) * 0.5
+        u[2, b, rows] = (outer - inner) * 0.5
 
 
 def windows(source, t, frames, k, rows):
@@ -113,7 +113,23 @@
                 acc[t, 1, 0:n] -= part
 
 
-def stem_kernel(
+def sum_phases(ws, phase):
+    spans = (((0,), (1, 2)), ((0, 1), (2,)))
+    for py in range(2):
+        for px in range(2):
+            for dy in range(2):
+                for dx in range(2):
+                    total = None
+                    for ty in spans[py][dy]:
+                        for tx in spans[px][dx]:
+                            term = ws[3 * ty + tx].astype(F32)
+                            total = term if total is None else total + term
+                    at = (2 * dy + dx) * C
+                    phase[2 * py + px, 0:CO, at : at + C] = total.astype(BF16)
+    phase[:, CO:256] = jnp.zeros((4, 256 - CO, 4 * C), BF16)
+
+
+def decode_kernel(
     lat_ref,
     arr_ref,
     we_hbm,
@@ -122,7 +138,8 @@
     g2_ref,
     w2_hbm,
     wt_hbm,
-    out_ref,
+    ws_hbm,
+    out_hbm,
     gath,
     lat4,
     late,
@@ -144,6 +161,12 @@
     u1,
     u2,
     wt,
+    ws,
+    phase,
+    wide,
+    low,
+    high,
+    ready,
     wsem,
     gsend,
     grecv,
@@ -152,6 +175,7 @@
     hrecv,
     ssend,
     srecv,
+    osem,
 ):
     seq = lax.axis_index("seq")
     band = lax.axis_index("tile")
@@ -170,6 +194,7 @@
             )
         )
     load_wt = pltpu.make_async_copy(wt_hbm, wt, wsem.at[27])
+    load_ws = pltpu.make_async_copy(ws_hbm, ws, wsem.at[28])
 
     barrier = pltpu.get_barrier_semaphore()
     for d in range(1, BANDS):
@@ -177,7 +202,7 @@
             barrier, inc=1, device_id=(seq, lax.rem(band + d, BANDS)), device_id_type=MESH
         )
     pl.semaphore_signal(barrier, inc=1, device_id=(mate, band), device_id_type=MESH)
-    for load in loads1 + loads0 + loads2 + [load_wt]:
+    for load in loads1 + loads0 + [load_ws] + loads2 + [load_wt]:
         load.start()
     pl.semaphore_wait(barrier, BANDS)
 
@@ -215,6 +240,8 @@
     for load in loads1:
         load.wait()
     combine_weights(u1)
+    load_ws.wait()
+    sum_phases(ws, phase)
 
     for push in pushes:
         push.wait_recv()
@@ -314,7 +341,7 @@
             v = mid[pl.ds(COLS * y, COLS)].astype(BF16)
             if 1 <= y <= ROWS:
                 first[t, y - 1] = v
-            h = silu_norm(v.astype(F32), g1_ref[...])
+            h = silu_norm(v.astype(F32), 0.5 * g1_ref[...])
             if y == 0:
                 h = h * has_up
             if y == TALL - 1:
@@ -344,26 +371,24 @@
 
     def activate(t, k, y, out=None):
         rows = pl.ds(HALF * k, HALF)
-        even = silu_norm(acc[t, 0, rows], g2_ref[...])
-        odd = silu_norm(acc[t, 1, rows], g2_ref[...])
+        even = silu_norm(acc[t, 0, rows], 0.5 * g2_ref[...])
+        odd = silu_norm(acc[t, 1, rows], 0.5 * g2_ref[...])
         put_row(h2, t, y + 1, even, odd)
         if out is not None:
             out[t, 0:HALF] = even.astype(BF16)
             out[t, HALF:] = odd.astype(BF16)
 
-    conv(h1, u1, acc, [far_row])
+    conv(h1, u1, acc, [far_row, near_row])
     for t in range(FRAMES):
         activate(t, 0, far_row, slow_out)
     halos = [push_to(slow_out, slow_in, far, hsend.at[0], hrecv.at[0])]
-    conv(h1, u1, acc, others)
-    for t in range(FRAMES):
-        for k in range(3):
-            activate(t, k, others[k])
-    for t in range(FRAMES):
-        rows = pl.ds(pl.multiple_of(2 * HALF * (1 - odd_band), HALF), HALF)
-        fast_out[t, 0:HALF] = silu_norm(acc[t, 0, rows], g2_ref[...]).astype(BF16)
-        fast_out[t, HALF:] = silu_norm(acc[t, 1, rows], g2_ref[...]).astype(BF16)
+    for t in range(FRAMES):
+        activate(t, 1, near_row, fast_out)
     halos.append(push_to(fast_out, fast_in, near, hsend.at[1], hrecv.at[1]))
+    conv(h1, u1, acc, [1, 2])
+    for t in range(FRAMES):
+        activate(t, 0, 1)
+        activate(t, 1, 2)
 
     def finish(t, k, y):
         rows = pl.ds(HALF * k, HALF)
@@ -372,6 +397,24 @@
             total = acc[t, par, rows] + first[t, y, cols].astype(F32)
             s_ref[t + 2, y + 1, cols] = total.astype(BF16)
 
+    frames = pl.ds(2, FRAMES)
+    halos[1].wait_recv()
+    for t in range(FRAMES):
+        h = fast_in[t].astype(F32)
+        put_row(h2, t, near_halo, h[0:HALF], h[HALF:])
+    conv(h2, u2, acc, others)
+    for t in range(FRAMES):
+        for k in range(3):
+            finish(t, k, others[k])
+    edges = [
+        push_to(
+            s_ref.at[frames, near_row + 1],
+            s_ref.at[frames, 5 - near_halo],
+            near,
+            ssend.at[1],
+            srecv.at[1],
+        )
+    ]
     halos[0].wait_recv()
     for t in range(FRAMES):
         h = slow_in[t].astype(F32) * far_inside
@@ -379,8 +422,7 @@
     conv(h2, u2, acc, [far_row])
     for t in range(FRAMES):
         finish(t, 0, far_row)
-    frames = pl.ds(2, FRAMES)
-    edges = [
+    edges.append(
         push_to(
             s_ref.at[frames, far_row + 1],
             s_ref.at[frames, 5 - far_halo],
@@ -388,53 +430,90 @@
             ssend.at[0],
             srecv.at[0],
         )
-    ]
-    halos[1].wait_recv()
-    for t in range(FRAMES):
-        h = fast_in[t].astype(F32)
-        put_row(h2, t, near_halo, h[0:HALF], h[HALF:])
-    conv(h2, u2, acc, others)
-    for t in range(FRAMES):
-        for k in range(3):
-            finish(t, k, others[k])
-    edges.append(
-        push_to(
-            s_ref.at[frames, near_row + 1],
-            s_ref.at[frames, 5 - near_halo],
-            near,
-            ssend.at[1],
-            srecv.at[1],
-        )
     )
-
-    load_wt.wait()
 
     def double(rows):
         cells = len(rows) * COLS
         stacked = jnp.concatenate(
             [
-                jnp.concatenate(
-                    [s_ref[BLOCK * half + i + a, y] for a in range(3)], axis=1
-                )
+                jnp.concatenate([s_ref[BLOCK * half + i + a, y] for a in range(3)], axis=1)
                 for i in range(BLOCK)
                 for y in rows
             ],
             axis=0,
         )
-        r = jnp.dot(stacked, wt[...], preferred_element_type=F32).astype(BF16)
+        r = jnp.dot(stacked, wt[...], preferred_element_type=F32)
         for i in range(BLOCK):
             for k, y in enumerate(rows):
-                at = i * cells + k * COLS
-                out_ref[2 * i, y] = r[at : at + COLS, 0:C]
-                out_ref[2 * i + 1, y] = r[at : at + COLS, C : 2 * C]
-
-    double(range(1, ROWS + 1))
-    for copy in edges:
-        copy.wait_recv()
+                for later in range(2):
+                    at = i * cells + k * COLS
+                    h = r[at : at + COLS, C * later : C * (later + 1)]
+                    even, odd = h[0:HALF], h[HALF:]
+                    f = 2 * i + later
+                    wide[f, y, :, 0:C] = before(odd).astype(BF16)
+                    wide[f, y, :, C : 2 * C] = even.astype(BF16)
+                    wide[f, y, :, 2 * C : 3 * C] = odd.astype(BF16)
+                    wide[f, y, :, 3 * C : 4 * C] = after(even).astype(BF16)
+
+    outs = []
+
+    def upsample(side, rows):
+        py = side + odd_band - 2 * side * odd_band
+        at_row = {y: y + odd_band * (3 - 2 * y) for y in rows}
+        for px in range(2):
+            window = jnp.concatenate(
+                [
+                    jnp.concatenate(
+                        [
+                            wide[f, at_row[y] + py + dy, :, C * (px + par) : C * (px + par + 2)]
+                            for dy in range(2)
+                        ],
+                        axis=1,
+                    )
+                    for f in range(2 * BLOCK)
+                    for y in rows
+                    for par in range(2)
+                ],
+                axis=0,
+            )
+            r = lax.dot_general(
+                window,
+                phase[2 * py + px],
+                (((1,), (1,)), ((), ())),
+                preferred_element_type=F32,
+            )
+            at = 0
+            for f in range(2 * BLOCK):
+                for y in rows:
+                    for par in range(2):
+                        cols = pl.ds(2 * par + px, HALF, 4)
+                        low[side, f, y, cols, :] = r[at : at + HALF, 0:128]
+                        high[side, f, y, cols, :] = r[at : at + HALF, 128:256]
+                        at += HALF
+        for f in range(2 * BLOCK):
+            for y in rows:
+                row = 2 * at_row[y] + py
+                ready[f, row, 0:128] = low[side, f, y].T.astype(BF16)
+                ready[f, row, 128:CO] = high[side, f, y].T[0 : CO - 128].astype(BF16)
+                copy = pltpu.make_async_copy(
+                    ready.at[f, row], out_hbm.at[f, row], osem.at[len(outs)]
+                )
+                copy.start()
+                outs.append(copy)
+
+    load_wt.wait()
+    edges[0].wait_recv()
+    double([1, 2, 3, 4, near_halo])
+    upsample(1, [0, 1, 2, 3])
+    upsample(0, [1, 2, 3])
+    edges[1].wait_recv()
     for t in range(FRAMES):
         s_ref[t + 2, far_halo] = (s_ref[t + 2, far_halo].astype(F32) * far_inside).astype(BF16)
-    double((0, TALL - 1))
-
+    double([far_halo])
+    upsample(0, [0])
+
+    for copy in outs:
+        copy.wait()
     for push in pushes:
         push.wait_send()
     swap.wait_send()
@@ -442,16 +521,16 @@
         copy.wait_send()
 
 
-def stem(lat, arr, we, g1, w1, g2, w2, wt):
+def decode(lat, arr, we, g1, w1, g2, w2, wt, ws):
     vmem = pl.BlockSpec(memory_space=pltpu.VMEM)
     smem = pl.BlockSpec(memory_space=pltpu.SMEM)
     hbm = pl.BlockSpec(memory_space=pl.ANY)
     dma = pltpu.SemaphoreType.DMA
     return pl.pallas_call(
-        stem_kernel,
-        out_shape=jax.ShapeDtypeStruct((2 * BLOCK, TALL, COLS, C), BF16),
-        in_specs=[vmem, smem, hbm, vmem, hbm, vmem, hbm, hbm],
-        out_specs=vmem,
+        decode_kernel,
+        out_shape=jax.ShapeDtypeStruct((2 * BLOCK, 2 * ROWS, CO, 2 * COLS), BF16),
+        in_specs=[vmem, smem, hbm, vmem, hbm, vmem, hbm, hbm, hbm],
+        out_specs=hbm,
         scratch_shapes=[
             pltpu.VMEM((2 * BANDS, ROWS, COLS * LAT), BF16),
             pltpu.VMEM((2, 16, COLS * LAT), BF16),
@@ -474,7 +553,13 @@
             pltpu.VMEM((4, 3, C, 3 * C), BF16),
             pltpu.VMEM((4, 3, C, 3 * C), BF16),
             pltpu.VMEM((3 * C, 2 * C), BF16),
-            dma((28,)),
+            pltpu.VMEM((9, CO, C), BF16),
+            pltpu.VMEM((4, 256, 4 * C), BF16),
+            pltpu.VMEM((2 * BLOCK, TALL, HALF, 4 * C), BF16),
+            pltpu.VMEM((2, 2 * BLOCK, ROWS, 2 * COLS, 128), F32),
+            pltpu.VMEM((2, 2 * BLOCK, ROWS, 2 * COLS, 128), F32),
+            pltpu.VMEM((2 * BLOCK, 2 * ROWS, CO, 2 * COLS), BF16),
+            dma((29,)),
             dma((BANDS,)),
             dma((BANDS,)),
             dma((2,)),
@@ -482,96 +567,13 @@
             dma((2,)),
             dma((2,)),
             dma((2,)),
+            dma((4 * BLOCK * ROWS,)),
         ],
         compiler_params=pltpu.CompilerParams(
-            collective_id=0, has_side_effects=True, vmem_limit_bytes=56 * 2**20
+            collective_id=0, has_side_effects=True, vmem_limit_bytes=60 * 2**20
         ),
-        name="stem",
-    )(lat, arr, we, g1, w1, g2, w2, wt)
-
-
-def upsample_kernel(d_ref, w_ref, out_ref, wide, phase, low, high):
-    @pl.when(pl.program_id(0) == 0)
-    def _():
-        spans = (((0,), (1, 2)), ((0, 1), (2,)))
-        for py in range(2):
-            for px in range(2):
-                for dy in range(2):
-                    for dx in range(2):
-                        total = None
-                        for ty in spans[py][dy]:
-                            for tx in spans[px][dx]:
-                                term = w_ref[3 * ty + tx].astype(F32)
-                                total = term if total is None else total + term
-                        at = (2 * dy + dx) * C
-                        phase[2 * py + px, 0:CO, at : at + C] = total.astype(BF16)
-        phase[:, CO:256] = jnp.zeros((4, 256 - CO, 4 * C), BF16)
-
-    frames = d_ref.shape[0]
-    for f in range(frames):
-        for y in range(TALL):
-            even, odd = d_ref[f, y, 0:HALF], d_ref[f, y, HALF:]
-            wide[f, y, :, 0:C] = before(odd.astype(F32)).astype(BF16)
-            wide[f, y, :, C : 2 * C] = even
-            wide[f, y, :, 2 * C : 3 * C] = odd
-            wide[f, y, :, 3 * C : 4 * C] = after(even.astype(F32)).astype(BF16)
-    for py in range(2):
-        for px in range(2):
-            window = jnp.concatenate(
-                [
-                    jnp.concatenate(
-                        [
-                            wide[f, y + py + dy, :, C * (px + par) : C * (px + par + 2)]
-                            for dy in range(2)
-                        ],
-                        axis=1,
-                    )
-                    for f in range(frames)
-                    for y in range(ROWS)
-                    for par in range(2)
-                ],
-                axis=0,
-            )
-            r = lax.dot_general(
-                window,
-                phase[2 * py + px],
-                (((1,), (1,)), ((), ())),
-                preferred_element_type=F32,
-            )
-            for f in range(frames):
-                for y in range(ROWS):
-                    for par in range(2):
-                        at = ((f * ROWS + y) * 2 + par) * HALF
-                        cols = pl.ds(2 * par + px, HALF, 4)
-                        low[f, y, py, cols, :] = r[at : at + HALF, 0:128]
-                        high[f, y, py, cols, :] = r[at : at + HALF, 128:256]
-    for f in range(frames):
-        for y in range(ROWS):
-            for py in range(2):
-                out_ref[f, 2 * y + py, 0:128] = low[f, y, py].T.astype(BF16)
-                out_ref[f, 2 * y + py, 128:CO] = high[f, y, py].T[0 : CO - 128].astype(BF16)
-
-
-def upsample(doubled, w):
-    frames = 2
-    return pl.pallas_call(
-        upsample_kernel,
-        grid=(2 * BLOCK // frames,),
-        out_shape=jax.ShapeDtypeStruct((2 * BLOCK, 2 * ROWS, CO, 2 * COLS), BF16),
-        in_specs=[
-            pl.BlockSpec((frames, TALL, COLS, C), lambda f: (f, 0, 0, 0)),
-            pl.BlockSpec((9, CO, C), lambda f: (0, 0, 0)),
-        ],
-        out_specs=pl.BlockSpec((frames, 2 * ROWS, CO, 2 * COLS), lambda f: (f, 0, 0, 0)),
-        scratch_shapes=[
-            pltpu.VMEM((frames, TALL, HALF, 4 * C), BF16),
-            pltpu.VMEM((4, 256, 4 * C), BF16),
-            pltpu.VMEM((frames, ROWS, 2, 2 * COLS, 128), F32),
-            pltpu.VMEM((frames, ROWS, 2, 2 * COLS, 128), F32),
-        ],
-        compiler_params=pltpu.CompilerParams(vmem_limit_bytes=60 * 2**20),
-        name="upsample",
-    )(doubled, w)
+        name="decode",
+    )(lat, arr, we, g1, w1, g2, w2, wt, ws)
 
 
 def local(
@@ -585,7 +587,7 @@
     temporal_upscale_weight,
     spatial_upscale_weight,
 ):
-    doubled = stem(
+    decoded = decode(
         transformer_latents,
         tile_arrangement,
         entry_conv_weight.reshape(27 * LAT, C),
@@ -594,9 +596,7 @@
         second_norm_gain,
         second_conv_weight,
         temporal_upscale_weight.reshape(3 * C, 2 * C),
-    )
-    decoded = upsample(
-        doubled, jnp.transpose(spatial_upscale_weight, (0, 1, 3, 2)).reshape(9, CO, C)
+        jnp.transpose(spatial_upscale_weight, (0, 1, 3, 2)).reshape(9, CO, C),
     )
     return jnp.transpose(decoded, (0, 1, 3, 2))
 

time: 50.9 us -> 47.5 us (0.933)
  Pallas kernels: 50.7 us -> 44.6 us
  local copies, waits for them, and re-layouts: 0 us -> 2.66 us
    pallas_call x2 -> x1, Pallas kernels: 50.7 us -> 44.6 us  [decode(): pl.pallas_call(decode_kernel, out_shape=jax.ShapeDtypeStruct((2 * BLOCK,...]
    unnamed x0 -> x1, local copies, waits for them, and re-layouts: none -> 2.66 us
where the time goes in v4:
time: 47.5 us; the launch traced here: 47.3 us
  Pallas kernels  44.6 us (94%)
  local copies, waits for them, and re-layouts  2.66 us (6%)
    pallas_call x1, Pallas kernels, decode(): pl.pallas_call(decode_kernel, out_shape=jax.ShapeDtypeStruct((2 * BLOCK,...  44.6 us
    unnamed x1, local copies, waits for them, and re-layouts  2.66 us

profile of v4, /device:TPU:1, one launch (start us, length us, event | category | flops | bytes accessed | tf_op | source)
XLA Modules:
  0.0 47.3 jit_solution(9623859579383634663)
XLA Ops:
  0.0 44.6 %decode.1 = bf16[4,8,192,128]{3,2,1,0:T(8,128)(2,1)} custom-call(bf16[2,4,1024]{2,1,0:T(4,128)(2,1)} %lat_ref.1, s32[1,32]{1,0:T(1,128)} %arr_ref.1, bf16[432,384]{1,0:T(8,128)(2,1)} %bitcast.9, f32[384]{0:T(512)} %g1_ref.1, bf16[3,3,3,384,384]{4,3,2,1,0:T(8,128)(2,1)} %w1_hbm.1, f32[384]{0:T(512)} %g2_ref.1, bf16[3,3,3,384,384]{4,3,2,1,0:T(8,128)(2,1)} %w2_hbm.1, ...), custom_call_target="tpu_custom_call" | custom-call | tf_op jit(solution)/shard_map/decode/pallas_call | solution.py:529
  44.6 2.7 %copy.11 = bf16[4,8,128,192]{2,3,1,0:T(8,128)(2,1)} copy(bf16[4,8,128,192]{2,3,1,0:T(8,128)(2,1)} %bitcast.6) | data formatting | bytes 3145728

commit v5 on v4

--- a/solution.py
+++ b/solution.py
@@ -270,51 +270,44 @@
     spread = (
         lax.rem(lax.broadcasted_iota(jnp.int32, (16, COLS * LAT), 1), 256) // LAT == column_of
     ).astype(F32)
-    kk = lax.broadcasted_iota(jnp.int32, (768, 256), 0)
-    nn = lax.broadcasted_iota(jnp.int32, (768, 256), 1)
-    want = jnp.where(nn < 128, nn, nn - 128 - 64)
-    place = (
-        (want >= 0)
-        & (want < 48)
-        & (want // LAT == kk // 256)
-        & (lax.rem(want, LAT) == lax.rem(kk, LAT))
-    )
-    place = place.astype(F32).astype(BF16)
+    kk = lax.broadcasted_iota(jnp.int32, (256, 128), 0)
+    nn = lax.broadcasted_iota(jnp.int32, (256, 128), 1)
+    place = (lax.rem(nn, LAT) == lax.rem(kk, LAT)).astype(F32).astype(BF16)
+    lane = lax.broadcasted_iota(jnp.int32, (HALF, 128), 1)
+    slot = lane // LAT
+
+    def taps(left, centre, right, base):
+        picked = jnp.where(slot == base + 1, centre, 0.0)
+        picked = jnp.where(slot == base, left, picked)
+        return jnp.where(slot == base + 2, right, picked).astype(BF16)
 
     def relayout(block):
-        lat = lat4[block].astype(F32)
-        lane = lax.broadcasted_iota(jnp.int32, lat.shape, 1)
-        late[0] = jnp.where(lane < LAT, 0.0, pltpu.roll(lat, LAT, 1))
-        late[1] = lat
-        late[2] = jnp.where(lane >= (COLS - 1) * LAT, 0.0, pltpu.roll(lat, (COLS - 1) * LAT, 1))
+        late[...] = lat4[block].astype(F32)
 
         @pl.loop(0, 16)
         def _(r):
-            for e in range(3):
-                row = late[e, pl.ds(r, 1), :]
-                full = (jnp.broadcast_to(row, (16, COLS * LAT)) * spread).astype(BF16)
-                for g in range(4):
-                    lhs[r, pl.ds(16 * g, 16), 256 * e : 256 * (e + 1)] = full[
-                        :, 256 * g : 256 * (g + 1)
-                    ]
-
-        @pl.loop(0, 2)
-        def _(i):
+            row = late[pl.ds(r, 1), :]
+            full = (jnp.broadcast_to(row, (16, COLS * LAT)) * spread).astype(BF16)
+            for g in range(4):
+                lhs[r, pl.ds(16 * g, 16)] = full[:, 256 * g : 256 * (g + 1)]
+
+        for i in range(2):
             r = jnp.dot(
-                lhs[pl.ds(8 * i, 8)].reshape(8 * COLS, 768), place, preferred_element_type=F32
-            )
-            r = jnp.concatenate(
-                [
-                    r[at : at + 8]
-                    for y in range(8)
+                lhs[pl.ds(8 * i, 8)].reshape(8 * COLS, 256), place, preferred_element_type=F32
+            )
+            t = 2 * block + i
+            for y in range(8):
+                even, odd = (
+                    jnp.concatenate(
+                        [r[at : at + 8] for at in range(y * COLS + 8 * par, (y + 1) * COLS, 16)],
+                        axis=0,
+                    )
                     for par in range(2)
-                    for at in range(y * COLS + 8 * par, (y + 1) * COLS, 16)
-                ],
-                axis=0,
-            ).astype(BF16)
-            t = 2 * block + i
-            rlo[t + 2] = r[:, 0:128].reshape(8, COLS, 128)
-            rhi[t + 2] = r[:, 128:256].reshape(8, COLS, 128)
+                )
+                left, right = before(odd), after(even)
+                for ref, base in ((rlo, 0), (rhi, 4)):
+                    ref[t + 2, y, 0:HALF] = taps(left, even, odd, base)
+                    ref[t + 2, y, HALF:] = taps(even, odd, right, base)
 
     relayout(half)
     for load in loads2:
@@ -534,8 +527,8 @@
         scratch_shapes=[
             pltpu.VMEM((2 * BANDS, ROWS, COLS * LAT), BF16),
             pltpu.VMEM((2, 16, COLS * LAT), BF16),
-            pltpu.VMEM((3, 16, COLS * LAT), F32),
-            pltpu.VMEM((16, COLS, 768), BF16),
+            pltpu.VMEM((16, COLS * LAT), F32),
+            pltpu.VMEM((16, COLS, 256), BF16),
             pltpu.VMEM((6, 8, COLS, 128), BF16),
             pltpu.VMEM((6, 8, COLS, 128), BF16),
             pltpu.VMEM((TALL * COLS, 640), BF16),
@@ -576,6 +569,32 @@
     )(lat, arr, we, g1, w1, g2, w2, wt, ws)
 
 
+def hand_over_kernel(src, dst, sems):
+    copies = []
+    for f in range(2 * BLOCK):
+        for part in range(4):
+            rows = pl.ds(2 * part, 2)
+            copies.append(
+                pltpu.make_async_copy(src.at[f, rows], dst.at[f, rows], sems.at[4 * f + part])
+            )
+    for copy in copies:
+        copy.start()
+    for copy in copies:
+        copy.wait()
+
+
+def hand_over(decoded):
+    return pl.pallas_call(
+        hand_over_kernel,
+        out_shape=jax.ShapeDtypeStruct(decoded.shape, decoded.dtype),
+        in_specs=[pl.BlockSpec(memory_space=pl.ANY)],
+        out_specs=pl.BlockSpec(memory_space=pl.ANY),
+        scratch_shapes=[pltpu.SemaphoreType.DMA((8 * BLOCK,))],
+        compiler_params=pltpu.CompilerParams(vmem_limit_bytes=63 * 2**20),
+        name="hand_over",
+    )(decoded)
+
+
 def local(
     transformer_latents,
     tile_arrangement,
@@ -598,7 +617,7 @@
         temporal_upscale_weight.reshape(3 * C, 2 * C),
         jnp.transpose(spatial_upscale_weight, (0, 1, 3, 2)).reshape(9, CO, C),
     )
-    return jnp.transpose(decoded, (0, 1, 3, 2))
+    return jnp.transpose(hand_over(decoded), (0, 1, 3, 2))
 
 
 def solution(mesh):

time: 47.5 us -> 92.8 us (1.95)
  Pallas kernels: 44.6 us -> 92.5 us
  local copies, waits for them, and re-layouts: 2.66 us -> 0 us
    pallas_call x0 -> x1, Pallas kernels: none -> 48.9 us  [hand_over(): pl.pallas_call(hand_over_kernel, out_shape=jax.ShapeDtypeStruct(decoded.s...]
    unnamed x1 -> x0, local copies, waits for them, and re-layouts: 2.66 us -> none
    pallas_call x1, Pallas kernels: 44.6 us -> 43.6 us  [decode(): pl.pallas_call(decode_kernel, out_shape=jax.ShapeDtypeStruct((2 * BLOCK,...]
where the time goes in v5:
time: 92.8 us; the launch traced here: 92.7 us
  Pallas kernels  92.5 us (100%)
    pallas_call x1, Pallas kernels, hand_over(): pl.pallas_call(hand_over_kernel, out_shape=jax.ShapeDtypeStruct(decoded.s...  48.9 us
    pallas_call x1, Pallas kernels, decode(): pl.pallas_call(decode_kernel, out_shape=jax.ShapeDtypeStruct((2 * BLOCK,...  43.6 us

profile of v5, /device:TPU:1, one launch (start us, length us, event | category | flops | bytes accessed | tf_op | source)
XLA Modules:
  0.0 92.7 jit_solution(15384071815242629318)
XLA Ops:
  0.0 43.6 %decode.1.src = bf16[4,8,192,128]{3,2,1,0:T(8,128)(2,1)} custom-call(bf16[2,4,1024]{2,1,0:T(4,128)(2,1)} %lat_ref.1, s32[1,32]{1,0:T(1,128)} %arr_ref.1, bf16[432,384]{1,0:T(8,128)(2,1)} %bitcast.8, f32[384]{0:T(512)} %g1_ref.1, bf16[3,3,3,384,384]{4,3,2,1,0:T(8,128)(2,1)} %w1_hbm.1, f32[384]{0:T(512)} %g2_ref.1, bf16[3,3,3,384,384]{4,3,2,1,0:T(8,128)(2,1)} %w2_hbm.1, ...), custom_call_target="tpu_custom_call" | custom-call | tf_op jit(solution)/shard_map/decode/pallas_call | solution.py:522
  43.6 48.9 %hand_over.1 = bf16[4,8,192,128]{3,2,1,0:T(8,128)(2,1)} custom-call(bf16[4,8,192,128]{3,2,1,0:T(8,128)(2,1)} %decode.1.src), custom_call_target="tpu_custom_call" | custom-call | tf_op jit(solution)/shard_map/hand_over/pallas_call | solution.py:587

commit v6 on v5

--- a/solution.py
+++ b/solution.py
@@ -130,16 +130,19 @@
 
 
 def decode_kernel(
-    lat_ref,
-    arr_ref,
+    lat_hbm,
+    arr_hbm,
     we_hbm,
-    g1_ref,
+    g1_hbm,
     w1_hbm,
-    g2_ref,
+    g2_hbm,
     w2_hbm,
     wt_hbm,
     ws_hbm,
-    out_hbm,
+    out_ref,
+    arr_ref,
+    g1_ref,
+    g2_ref,
     gath,
     lat4,
     late,
@@ -166,7 +169,6 @@
     wide,
     low,
     high,
-    ready,
     wsem,
     gsend,
     grecv,
@@ -175,7 +177,6 @@
     hrecv,
     ssend,
     srecv,
-    osem,
 ):
     seq = lax.axis_index("seq")
     band = lax.axis_index("tile")
@@ -194,6 +195,11 @@
             )
         )
     load_wt = pltpu.make_async_copy(wt_hbm, wt, wsem.at[27])
+    load_arr = pltpu.make_async_copy(arr_hbm, arr_ref, wsem.at[32])
+    load_gains = [
+        pltpu.make_async_copy(g1_hbm, g1_ref, wsem.at[30]),
+        pltpu.make_async_copy(g2_hbm, g2_ref, wsem.at[31]),
+    ]
     load_ws = pltpu.make_async_copy(ws_hbm, ws, wsem.at[28])
 
     barrier = pltpu.get_barrier_semaphore()
@@ -202,7 +208,7 @@
             barrier, inc=1, device_id=(seq, lax.rem(band + d, BANDS)), device_id_type=MESH
         )
     pl.semaphore_signal(barrier, inc=1, device_id=(mate, band), device_id_type=MESH)
-    for load in loads1 + loads0 + [load_ws] + loads2 + [load_wt]:
+    for load in [load_arr] + load_gains + loads1 + loads0 + [load_ws] + loads2 + [load_wt]:
         load.start()
     pl.semaphore_wait(barrier, BANDS)
 
@@ -210,7 +216,7 @@
     for d in range(1, BANDS):
         pushes.append(
             pltpu.make_async_remote_copy(
-                src_ref=lat_ref,
+                src_ref=lat_hbm,
                 dst_ref=gath.at[pl.ds(2 * band, 2)],
                 send_sem=gsend.at[d],
                 recv_sem=grecv.at[d],
@@ -220,7 +226,9 @@
         )
     for push in pushes:
         push.start()
-    gath[pl.ds(2 * band, 2)] = lat_ref[...]
+    load_own = pltpu.make_async_copy(lat_hbm, gath.at[pl.ds(2 * band, 2)], wsem.at[29])
+    load_own.start()
+    load_own.wait()
 
     for p in range(9):
         we[pl.ds(64 * p + 48, 16)] = jnp.zeros((16, C), BF16)
@@ -228,6 +236,7 @@
     rlo[0:2] = jnp.zeros((2, 8, COLS, 128), BF16)
     rhi[0:2] = jnp.zeros((2, 8, COLS, 128), BF16)
     s_ref[0:2] = jnp.zeros((2, TALL, COLS, C), BF16)
+    load_arr.wait()
     spots = []
     for i in range(BLOCK):
         for o in (-1, 0, 1):
@@ -316,7 +325,7 @@
     swap.wait_recv()
     relayout(1 - half)
 
-    for load in loads0:
+    for load in load_gains + loads0:
         load.wait()
 
     @pl.loop(0, 4)
@@ -447,8 +456,6 @@
                     wide[f, y, :, C : 2 * C] = even.astype(BF16)
                     wide[f, y, :, 2 * C : 3 * C] = odd.astype(BF16)
                     wide[f, y, :, 3 * C : 4 * C] = after(even).astype(BF16)
-
-    outs = []
 
     def upsample(side, rows):
         py = side + odd_band - 2 * side * odd_band
@@ -486,13 +493,8 @@
         for f in range(2 * BLOCK):
             for y in rows:
                 row = 2 * at_row[y] + py
-                ready[f, row, 0:128] = low[side, f, y].T.astype(BF16)
-                ready[f, row, 128:CO] = high[side, f, y].T[0 : CO - 128].astype(BF16)
-                copy = pltpu.make_async_copy(
-                    ready.at[f, row], out_hbm.at[f, row], osem.at[len(outs)]
-                )
-                copy.start()
-                outs.append(copy)
+                out_ref[f, row, 0:128] = low[side, f, y].T.astype(BF16)
+                out_ref[f, row, 128:CO] = high[side, f, y].T[0 : CO - 128].astype(BF16)
 
     load_wt.wait()
     edges[0].wait_recv()
@@ -505,8 +507,6 @@
     double([far_halo])
     upsample(0, [0])
 
-    for copy in outs:
-        copy.wait()
     for push in pushes:
         push.wait_send()
     swap.wait_send()
@@ -515,16 +515,17 @@
 
 
 def decode(lat, arr, we, g1, w1, g2, w2, wt, ws):
-    vmem = pl.BlockSpec(memory_space=pltpu.VMEM)
-    smem = pl.BlockSpec(memory_space=pltpu.SMEM)
-    hbm = pl.BlockSpec(memory_space=pl.ANY)
+    hbm = pl.BlockSpec(memory_space=pltpu.HBM)
     dma = pltpu.SemaphoreType.DMA
     return pl.pallas_call(
         decode_kernel,
         out_shape=jax.ShapeDtypeStruct((2 * BLOCK, 2 * ROWS, CO, 2 * COLS), BF16),
-        in_specs=[vmem, smem, hbm, vmem, hbm, vmem, hbm, hbm, hbm],
-        out_specs=hbm,
+        in_specs=[hbm] * 9,
+        out_specs=pl.BlockSpec(memory_space=pltpu.VMEM),
         scratch_shapes=[
+            pltpu.SMEM((1, 2 * BANDS), jnp.int32),
+            pltpu.VMEM((C,), F32),
+            pltpu.VMEM((C,), F32),
             pltpu.VMEM((2 * BANDS, ROWS, COLS * LAT), BF16),
             pltpu.VMEM((2, 16, COLS * LAT), BF16),
             pltpu.VMEM((16, COLS * LAT), F32),
@@ -551,8 +552,7 @@
             pltpu.VMEM((2 * BLOCK, TALL, HALF, 4 * C), BF16),
             pltpu.VMEM((2, 2 * BLOCK, ROWS, 2 * COLS, 128), F32),
             pltpu.VMEM((2, 2 * BLOCK, ROWS, 2 * COLS, 128), F32),
-            pltpu.VMEM((2 * BLOCK, 2 * ROWS, CO, 2 * COLS), BF16),
-            dma((29,)),
+            dma((33,)),
             dma((BANDS,)),
             dma((BANDS,)),
             dma((2,)),
@@ -560,39 +560,12 @@
             dma((2,)),
             dma((2,)),
             dma((2,)),
-            dma((4 * BLOCK * ROWS,)),
         ],
         compiler_params=pltpu.CompilerParams(
-            collective_id=0, has_side_effects=True, vmem_limit_bytes=60 * 2**20
+            collective_id=0, has_side_effects=True, vmem_limit_bytes=50 * 2**20
         ),
         name="decode",
     )(lat, arr, we, g1, w1, g2, w2, wt, ws)
-
-
-def hand_over_kernel(src, dst, sems):
-    copies = []
-    for f in range(2 * BLOCK):
-        for part in range(4):
-            rows = pl.ds(2 * part, 2)
-            copies.append(
-                pltpu.make_async_copy(src.at[f, rows], dst.at[f, rows], sems.at[4 * f + part])
-            )
-    for copy in copies:
-        copy.start()
-    for copy in copies:
-        copy.wait()
-
-
-def hand_over(decoded):
-    return pl.pallas_call(
-        hand_over_kernel,
-        out_shape=jax.ShapeDtypeStruct(decoded.shape, decoded.dtype),
-        in_specs=[pl.BlockSpec(memory_space=pl.ANY)],
-        out_specs=pl.BlockSpec(memory_space=pl.ANY),
-        scratch_shapes=[pltpu.SemaphoreType.DMA((8 * BLOCK,))],
-        compiler_params=pltpu.CompilerParams(vmem_limit_bytes=63 * 2**20),
-        name="hand_over",
-    )(decoded)
 
 
 def local(
@@ -606,18 +579,19 @@
     temporal_upscale_weight,
     spatial_upscale_weight,
 ):
+    pin = functools.partial(pltpu.with_memory_space_constraint, memory_space=pltpu.HBM)
     decoded = decode(
-        transformer_latents,
-        tile_arrangement,
-        entry_conv_weight.reshape(27 * LAT, C),
-        first_norm_gain,
+        pin(transformer_latents),
+        pin(tile_arrangement),
+        pin(entry_conv_weight.reshape(27 * LAT, C)),
+        pin(first_norm_gain),
         first_conv_weight,
-        second_norm_gain,
+        pin(second_norm_gain),
         second_conv_weight,
-        temporal_upscale_weight.reshape(3 * C, 2 * C),
-        jnp.transpose(spatial_upscale_weight, (0, 1, 3, 2)).reshape(9, CO, C),
+        pin(temporal_upscale_weight.reshape(3 * C, 2 * C)),
+        pin(jnp.transpose(spatial_upscale_weight, (0, 1, 3, 2)).reshape(9, CO, C)),
     )
-    return jnp.transpose(hand_over(decoded), (0, 1, 3, 2))
+    return jnp.transpose(decoded, (0, 1, 3, 2))
 
 
 def solution(mesh):

time: 92.8 us -> 43.6 us (0.47)
  Pallas kernels: 92.5 us -> 42.3 us
  local copies, waits for them, and re-layouts: 0 us -> 1.15 us
    pallas_call x1 -> x0, Pallas kernels: 48.9 us -> none  [hand_over(): pl.pallas_call(hand_over_kernel, out_shape=jax.ShapeDtypeStruct(decoded.s...]
    pallas_call x1, Pallas kernels: 43.6 us -> 42.3 us  [decode(): pl.pallas_call(decode_kernel, out_shape=jax.ShapeDtypeStruct((2 * BLOCK,...]
    unnamed x0 -> x1, local copies, waits for them, and re-layouts: none -> 1.15 us
where the time goes in v6:
time: 43.6 us; the launch traced here: 43.4 us
  Pallas kernels  42.3 us (97%)
  local copies, waits for them, and re-layouts  1.15 us (3%)
    pallas_call x1, Pallas kernels, decode(): pl.pallas_call(decode_kernel, out_shape=jax.ShapeDtypeStruct((2 * BLOCK,...  42.3 us
    unnamed x1, local copies, waits for them, and re-layouts  1.15 us

profile of v6, /device:TPU:1, one launch (start us, length us, event | category | flops | bytes accessed | tf_op | source)
XLA Modules:
  0.0 43.4 jit_solution(11730586791715562127)
XLA Ops:
  0.0 42.3 %decode.1 = bf16[4,8,192,128]{3,2,1,0:T(8,128)(2,1)S(1)} custom-call(bf16[2,4,1024]{2,1,0:T(4,128)(2,1)} %lat_hbm.1, s32[1,32]{1,0:T(1,128)} %arr_hbm.1, bf16[432,384]{1,0:T(8,128)(2,1)} %bitcast.9, f32[384]{0:T(512)} %g1_hbm.1, bf16[3,3,3,384,384]{4,3,2,1,0:T(8,128)(2,1)} %w1_hbm.1, f32[384]{0:T(512)} %g2_hbm.1, bf16[3,3,3,384,384]{4,3,2,1,0:T(8,128)(2,1)} %w2_hbm.1, ...), custom_call_target="tpu_custom_call" | custom-call | tf_op jit(solution)/shard_map/decode/pallas_call | solution.py:520
  42.3 1.1 %copy.11 = bf16[4,8,128,192]{2,3,1,0:T(8,128)(2,1)} copy(bf16[4,8,128,192]{2,3,1,0:T(8,128)(2,1)S(1)} %bitcast.6) | data formatting | bytes 3145728

commit v7 on v6

--- a/solution.py
+++ b/solution.py
@@ -83,34 +83,33 @@
     )
 
 
-def conv(source, u, acc, rows):
+def add(acc, t, k, n, part, fresh):
+    if k < 3:
+        acc[t, 0, 0:n] = part if fresh and k == 0 else acc[t, 0, 0:n] + part
+    if k == 1:
+        acc[t, 1, 0:n] = part if fresh else acc[t, 1, 0:n] + part
+    elif k > 1:
+        acc[t, 1, 0:n] -= part
+
+
+def conv(source, u, acc, rows, between=None):
     n = HALF * len(rows)
     for k in range(4):
         weight = u[k].reshape(3 * C, 3 * C)
-        if len(rows) == 1:
-            r = jnp.dot(windows(source, 0, 4, k, rows), weight, preferred_element_type=F32)
-            q = [r[n * i : n * (i + 1)] for i in range(4)]
-        else:
-            r = jnp.dot(windows(source, 0, 2, k, rows), weight, preferred_element_type=F32)
-            q = [r[0:n], r[n:]]
-            r = jnp.dot(
-                windows(source, 2, 2, k, rows), weight[:, 0 : 2 * C], preferred_element_type=F32
-            )
-            q += [r[0:n], r[n:]]
-        for t in range(FRAMES):
-            part = q[t][:, 0:C]
-            for back in range(1, min(t, 2) + 1):
-                part = part + q[t - back][:, back * C : (back + 1) * C]
-            if k == 0:
-                acc[t, 0, 0:n] = part
-            elif k == 1:
-                acc[t, 0, 0:n] += part
-                acc[t, 1, 0:n] = part
-            elif k == 2:
-                acc[t, 0, 0:n] += part
-                acc[t, 1, 0:n] -= part
-            else:
-                acc[t, 1, 0:n] -= part
+        r = jnp.dot(windows(source, 0, 2, k, rows), weight, preferred_element_type=F32)
+        a, b = r[0:n], r[n:]
+        add(acc, 0, k, n, a[:, 0:C], True)
+        add(acc, 1, k, n, a[:, C : 2 * C] + b[:, 0:C], True)
+        add(acc, 2, k, n, a[:, 2 * C :] + b[:, C : 2 * C], True)
+        add(acc, 3, k, n, b[:, 2 * C :], True)
+    if between is not None:
+        between()
+    for k in range(4):
+        weight = u[k].reshape(3 * C, 3 * C)[:, 0 : 2 * C]
+        r = jnp.dot(windows(source, 2, 2, k, rows), weight, preferred_element_type=F32)
+        a, b = r[0:n], r[n:]
+        add(acc, 2, k, n, a[:, 0:C], False)
+        add(acc, 3, k, n, a[:, C:] + b[:, 0:C], False)
 
 
 def sum_phases(ws, phase):
@@ -357,7 +356,6 @@
     near_row = 3 - far_row
     far_halo = 5 * odd_band
     near_halo = 5 - far_halo
-    others = [1 - odd_band + i for i in range(3)]
 
     def push_to(src, dst, to, send, recv):
         copy = pltpu.make_async_remote_copy(
@@ -380,13 +378,22 @@
             out[t, 0:HALF] = even.astype(BF16)
             out[t, HALF:] = odd.astype(BF16)
 
-    conv(h1, u1, acc, [far_row, near_row])
-    for t in range(FRAMES):
-        activate(t, 0, far_row, slow_out)
-    halos = [push_to(slow_out, slow_in, far, hsend.at[0], hrecv.at[0])]
-    for t in range(FRAMES):
-        activate(t, 1, near_row, fast_out)
-    halos.append(push_to(fast_out, fast_in, near, hsend.at[1], hrecv.at[1]))
+    outer = [far_row, near_row]
+    far_halos, far_edges = [], []
+
+    def send_hidden(t):
+        for i in range(2):
+            activate(t + i, 0, far_row, slow_out)
+        some = pl.ds(t, 2)
+        far_halos.append(
+            push_to(slow_out.at[some], slow_in.at[some], far, hsend.at[t], hrecv.at[t])
+        )
+        for i in range(2):
+            activate(t + i, 1, near_row, fast_out)
+
+    conv(h1, u1, acc, outer, lambda: send_hidden(0))
+    send_hidden(2)
+    near_halos = push_to(fast_out, fast_in, near, hsend.at[1], hrecv.at[1])
     conv(h1, u1, acc, [1, 2])
     for t in range(FRAMES):
         activate(t, 0, 1)
@@ -399,39 +406,51 @@
             total = acc[t, par, rows] + first[t, y, cols].astype(F32)
             s_ref[t + 2, y + 1, cols] = total.astype(BF16)
 
-    frames = pl.ds(2, FRAMES)
-    halos[1].wait_recv()
+    def take_far(t):
+        far_halos[t // 2].wait_recv()
+        for i in range(2):
+            h = slow_in[t + i].astype(F32) * far_inside
+            put_row(h2, t + i, far_halo, h[0:HALF], h[HALF:])
+
+    def send_second(t):
+        for i in range(2):
+            finish(t + i, 0, far_row)
+        some = pl.ds(t + 2, 2)
+        far_edges.append(
+            push_to(
+                s_ref.at[some, far_row + 1],
+                s_ref.at[some, 5 - far_halo],
+                far,
+                ssend.at[t],
+                srecv.at[t],
+            )
+        )
+        for i in range(2):
+            finish(t + i, 1, near_row)
+
+    conv(h2, u2, acc, [1, 2])
+    for t in range(FRAMES):
+        finish(t, 0, 1)
+        finish(t, 1, 2)
+    near_halos.wait_recv()
     for t in range(FRAMES):
         h = fast_in[t].astype(F32)
         put_row(h2, t, near_halo, h[0:HALF], h[HALF:])
-    conv(h2, u2, acc, others)
-    for t in range(FRAMES):
-        for k in range(3):
-            finish(t, k, others[k])
-    edges = [
-        push_to(
-            s_ref.at[frames, near_row + 1],
-            s_ref.at[frames, 5 - near_halo],
-            near,
-            ssend.at[1],
-            srecv.at[1],
-        )
-    ]
-    halos[0].wait_recv()
-    for t in range(FRAMES):
-        h = slow_in[t].astype(F32) * far_inside
-        put_row(h2, t, far_halo, h[0:HALF], h[HALF:])
-    conv(h2, u2, acc, [far_row])
-    for t in range(FRAMES):
-        finish(t, 0, far_row)
-    edges.append(
-        push_to(
-            s_ref.at[frames, far_row + 1],
-            s_ref.at[frames, 5 - far_halo],
-            far,
-            ssend.at[0],
-            srecv.at[0],
-        )
+    take_far(0)
+
+    def middle():
+        send_second(0)
+        take_far(2)
+
+    conv(h2, u2, acc, outer, middle)
+    send_second(2)
+    frames = pl.ds(2, FRAMES)
+    near_edges = push_to(
+        s_ref.at[frames, near_row + 1],
+        s_ref.at[frames, 5 - near_halo],
+        near,
+        ssend.at[1],
+        srecv.at[1],
     )
 
     def double(rows):
@@ -497,11 +516,13 @@
                 out_ref[f, row, 128:CO] = high[side, f, y].T[0 : CO - 128].astype(BF16)
 
     load_wt.wait()
-    edges[0].wait_recv()
-    double([1, 2, 3, 4, near_halo])
+    double([1, 2, 3, 4])
+    near_edges.wait_recv()
+    double([near_halo])
     upsample(1, [0, 1, 2, 3])
     upsample(0, [1, 2, 3])
-    edges[1].wait_recv()
+    for copy in far_edges:
+        copy.wait_recv()
     for t in range(FRAMES):
         s_ref[t + 2, far_halo] = (s_ref[t + 2, far_halo].astype(F32) * far_inside).astype(BF16)
     double([far_halo])
@@ -510,7 +531,7 @@
     for push in pushes:
         push.wait_send()
     swap.wait_send()
-    for copy in halos + edges:
+    for copy in far_halos + far_edges + [near_halos, near_edges]:
         copy.wait_send()
 
 
@@ -556,10 +577,10 @@
             dma((BANDS,)),
             dma((BANDS,)),
             dma((2,)),
-            dma((2,)),
-            dma((2,)),
-            dma((2,)),
-            dma((2,)),
+            dma((3,)),
+            dma((3,)),
+            dma((3,)),
+            dma((3,)),
         ],
         compiler_params=pltpu.CompilerParams(
             collective_id=0, has_side_effects=True, vmem_limit_bytes=50 * 2**20

time: 43.6 us -> 42 us (0.963)
  Pallas kernels: 42.3 us -> 40.7 us
    pallas_call x1, Pallas kernels: 42.3 us -> 40.7 us  [decode(): pl.pallas_call(decode_kernel, out_shape=jax.ShapeDtypeStruct((2 * BLOCK,...]
where the time goes in v7:
time: 42 us; the launch traced here: 41.8 us
  Pallas kernels  40.7 us (97%)
  local copies, waits for them, and re-layouts  1.15 us (3%)
    pallas_call x1, Pallas kernels, decode(): pl.pallas_call(decode_kernel, out_shape=jax.ShapeDtypeStruct((2 * BLOCK,...  40.7 us
    unnamed x1, local copies, waits for them, and re-layouts  1.15 us

profile of v7, /device:TPU:1, one launch (start us, length us, event | category | flops | bytes accessed | tf_op | source)
XLA Modules:
  0.0 41.8 jit_solution(832650015832291993)
XLA Ops:
  0.0 40.7 %decode.1 = bf16[4,8,192,128]{3,2,1,0:T(8,128)(2,1)S(1)} custom-call(bf16[2,4,1024]{2,1,0:T(4,128)(2,1)} %lat_hbm.1, s32[1,32]{1,0:T(1,128)} %arr_hbm.1, bf16[432,384]{1,0:T(8,128)(2,1)} %bitcast.9, f32[384]{0:T(512)} %g1_hbm.1, bf16[3,3,3,384,384]{4,3,2,1,0:T(8,128)(2,1)} %w1_hbm.1, f32[384]{0:T(512)} %g2_hbm.1, bf16[3,3,3,384,384]{4,3,2,1,0:T(8,128)(2,1)} %w2_hbm.1, ...), custom_call_target="tpu_custom_call" | custom-call | tf_op jit(solution)/shard_map/decode/pallas_call | solution.py:541
  40.7 1.1 %copy.11 = bf16[4,8,128,192]{2,3,1,0:T(8,128)(2,1)} copy(bf16[4,8,128,192]{2,3,1,0:T(8,128)(2,1)S(1)} %bitcast.6) | data formatting | bytes 3145728

commit v8 on v7

--- a/solution.py
+++ b/solution.py
@@ -148,8 +148,6 @@
     lhs,
     rlo,
     rhi,
-    patch,
-    mid,
     first,
     h1,
     h2,
@@ -327,19 +325,21 @@
     for load in load_gains + loads0:
         load.wait()
 
-    @pl.loop(0, 4)
-    def _(t):
-        taps = [(a, b) for a in range(3) for b in range(3)]
+    spans = [(a, b) for a in range(3) for b in range(3)]
+    for t in range(FRAMES):
+        parts = []
         for q in range(5):
-            a, b = taps[2 * q]
-            v = rlo[t + a, pl.ds(b, TALL)]
+            a, b = spans[2 * q]
+            v = rlo[t + a, b : b + TALL]
             if 2 * q + 1 < 9:
-                a, b = taps[2 * q + 1]
-                v = v + rhi[t + a, pl.ds(b, TALL)]
-            patch[:, 128 * q : 128 * (q + 1)] = v.reshape(TALL * COLS, 128)
-        mid[...] = jnp.dot(patch[...], we[...], preferred_element_type=F32)
+                a, b = spans[2 * q + 1]
+                v = v + rhi[t + a, b : b + TALL]
+            parts.append(v.reshape(TALL * COLS, 128))
+        entry = jnp.dot(
+            jnp.concatenate(parts, axis=1), we[...], preferred_element_type=F32
+        ).astype(BF16)
         for y in range(TALL):
-            v = mid[pl.ds(COLS * y, COLS)].astype(BF16)
+            v = entry[COLS * y : COLS * (y + 1)]
             if 1 <= y <= ROWS:
                 first[t, y - 1] = v
             h = silu_norm(v.astype(F32), 0.5 * g1_ref[...])
@@ -553,8 +553,6 @@
             pltpu.VMEM((16, COLS, 256), BF16),
             pltpu.VMEM((6, 8, COLS, 128), BF16),
             pltpu.VMEM((6, 8, COLS, 128), BF16),
-            pltpu.VMEM((TALL * COLS, 640), BF16),
-            pltpu.VMEM((TALL * COLS, C), F32),
             pltpu.VMEM((FRAMES, ROWS, COLS, C), BF16),
             pltpu.VMEM((FRAMES, TALL, 4, HALF, C), BF16),
             pltpu.VMEM((FRAMES, TALL, 4, HALF, C), BF16),

time: 42 us -> 41 us (0.976)
  Pallas kernels: 40.7 us -> 39.6 us
    pallas_call x1, Pallas kernels: 40.7 us -> 39.6 us  [decode(): pl.pallas_call(decode_kernel, out_shape=jax.ShapeDtypeStruct((2 * BLOCK,...]
where the time goes in v8:
time: 41 us; the launch traced here: 40.8 us
  Pallas kernels  39.6 us (97%)
  local copies, waits for them, and re-layouts  1.15 us (3%)
    pallas_call x1, Pallas kernels, decode(): pl.pallas_call(decode_kernel, out_shape=jax.ShapeDtypeStruct((2 * BLOCK,...  39.6 us
    unnamed x1, local copies, waits for them, and re-layouts  1.15 us

profile of v8, /device:TPU:1, one launch (start us, length us, event | category | flops | bytes accessed | tf_op | source)
XLA Modules:
  0.0 40.8 jit_solution(12911726423881531887)
XLA Ops:
  0.0 39.6 %decode.1 = bf16[4,8,192,128]{3,2,1,0:T(8,128)(2,1)S(1)} custom-call(bf16[2,4,1024]{2,1,0:T(4,128)(2,1)} %lat_hbm.1, s32[1,32]{1,0:T(1,128)} %arr_hbm.1, bf16[432,384]{1,0:T(8,128)(2,1)} %bitcast.9, f32[384]{0:T(512)} %g1_hbm.1, bf16[3,3,3,384,384]{4,3,2,1,0:T(8,128)(2,1)} %w1_hbm.1, f32[384]{0:T(512)} %g2_hbm.1, bf16[3,3,3,384,384]{4,3,2,1,0:T(8,128)(2,1)} %w2_hbm.1, ...), custom_call_target="tpu_custom_call" | custom-call | tf_op jit(solution)/shard_map/decode/pallas_call | solution.py:541
  39.6 1.1 %copy.11 = bf16[4,8,128,192]{2,3,1,0:T(8,128)(2,1)} copy(bf16[4,8,128,192]{2,3,1,0:T(8,128)(2,1)S(1)} %bitcast.6) | data formatting | bytes 3145728
